TPU v7x, 128 devices: a whole 4x4x4 slice. The times are simulated.
128 devices in a mesh: dom: 32 (over z, y, core), sub: 4 (over x).
Axes of the slice: x: 4, y: 4, z: 4, core: 2. Of those that a mesh axis runs over, the one named last changes fastest.
Arguments:
- velocity: float32 [5, 1048576], P(None, ('dom', 'sub')), may hold values from -6 to 6
- position: float32 [3, 1048576], P(None, ('dom', 'sub')), may hold values from 0 to 1
- inv_mass: float32 [1048576], P(('dom', 'sub')), may hold values from 0.05 to 0.3
- connectivity: int32 [4, 1048576], P(None, ('dom', 'sub')), may hold values from 0 to 8447, as said below
- shape_grad: float32 [2, 4, 1048576], P(None, None, ('dom', 'sub')), may hold values from -3 to 3
- area: float32 [1048576], P(('dom', 'sub')), may hold values from 0.5 to 2
- thickness: float32 [1048576], P(('dom', 'sub')), may hold values from 0.5 to 1.5
- yield_stress: float32 [1048576], P(('dom', 'sub')), may hold values from 0.5 to 3
- stress: float32 [5, 5, 1048576], P(None, None, ('dom', 'sub')), may hold values from -6 to 6
- contact_owner: int32 [1048576, 1], P(('dom', 'sub')), may hold values from 0 to 127; in each aligned block of 8192 rows (0 to 8191, 8192 to 16383, ...) at most 128 rows name the same one
- face_center: float32 [3, 262144], P(None, ('dom', 'sub')), may hold values from 0 to 1
- face_angle: float32 [2, 262144], P(None, ('dom', 'sub')), may hold values from -3.140625 to 3.140625
- face_stiffness: float32 [262144], P(('dom', 'sub')), may hold values from 1 to 10
- ghost_list: int32 [65536], P(('dom', 'sub')), may hold values from 0 to 2047
- pair_node: int32 [16384], P(('dom', 'sub')), may hold values from 0 to 127
- pair_face: int32 [16384], P(('dom', 'sub')), may hold values from 0 to 19
- pair_count: int32 [128], P(('dom', 'sub')), may hold values from 16 to 128, as said below
Outputs:
- new_velocity: float32 [5, 1048576], P(None, ('dom', 'sub'))
- new_stress: float32 [5, 5, 1048576], P(None, None, ('dom', 'sub'))
Inputs may be any that keep to these rules, and one draw needn't show every extreme that they name: `connectivity`: the corners of the element at local index e of a device lie in e .. e + 256; on the first device at least 128, on the last below 8320. `contact_owner`: the 8192 nodes of one device name any one contact device at most 128 times; some device reaches 128. `pair_count`: some device's count is 128 in every draw.
All inputs are finite; a program needn't handle non-finite values.
Results may differ from a plain program's by a relative error of at most 0.0003.
Values sent between devices are 32-bit elements; how exact they have to be, the bound alone decides.
A program may use at most 128 MiB of HBM per device.

v0:
```python
import math

import jax
import jax.numpy as jnp
from jax import lax
from jax.sharding import PartitionSpec as P

TILE = 128
HALO = 128
GHOST = 256


LOBATTO_POINTS = (-1.0, -0.6546536707079771, 0.0, 0.6546536707079771, 1.0)
LOBATTO_WEIGHTS = (0.1, 49.0 / 90.0, 32.0 / 45.0, 49.0 / 90.0, 0.1)
PLANE_MODULUS = 1.0 / 0.91
POISSON = 0.3
SHEAR_MODULUS = 5.0 / 6.0 / 2.6
DAMPING = 0.3
REACH_SQ = 0.5


def extended_2(x, sides, width):
    edges = {}
    for axis, dim in sides:
        count, length = (lax.axis_size(axis), x.shape[dim])
        up = [(i, (i + 1) % count) for i in range(count - 1)]
        last = lax.slice_in_dim(x, length - width, length, axis=dim)
        first = lax.slice_in_dim(x, 0, width, axis=dim)
        edges[dim] = (
            lax.ppermute(last, axis, up),
            lax.ppermute(first, axis, [(b, a) for a, b in up]),
        )
    done = []
    for _, dim in sides:
        low, high = edges[dim]
        around = [(width, width) if d in done else (0, 0) for d in range(x.ndim)]
        x = jnp.concatenate([jnp.pad(low, around), x, jnp.pad(high, around)], axis=dim)
        done.append(dim)
    return x


def in_blocks(x, dim, count):
    before, after = (x.shape[:dim], x.shape[dim + 1 :])
    return jnp.moveaxis(x.reshape(*before, count, -1, *after), dim, 0)


def joined_along(blocks, dim):
    blocks = jnp.moveaxis(blocks, 0, dim)
    lengths = blocks.shape
    return blocks.reshape(*lengths[:dim], lengths[dim] * lengths[dim + 1], *lengths[dim + 2 :])


def one_exchange(x, axis, axes, splits, concats):
    sizes = [lax.axis_size(a) for a in axes]
    blocks = in_blocks(x, splits[0], sizes[0])
    blocks = jnp.moveaxis(in_blocks(blocks, splits[1] + 1, sizes[1]), 0, 1)
    inside = blocks.shape[2:]
    blocks = blocks.reshape(-1, *inside)
    blocks = lax.all_to_all(blocks, axis, split_axis=0, concat_axis=0, tiled=True)
    blocks = joined_along(blocks.reshape(*sizes, *inside), concats[0] + 1)
    return joined_along(blocks, concats[1])


def element_forces(corner, grads, area, thickness, yield_stress, old_stress):
    vel_x, vel_y, vel_z, rot_x, rot_y = (corner[0], corner[1], corner[2], corner[3], corner[4])
    grad_x, grad_y = (grads[0], grads[1])
    memb_xx = jnp.sum(grad_x * vel_x, axis=0)
    bend_xx = jnp.sum(grad_x * rot_y, axis=0)
    memb_yy = jnp.sum(grad_y * vel_y, axis=0)
    bend_yy = -jnp.sum(grad_y * rot_x, axis=0)
    memb_xy = jnp.sum(grad_y * vel_x + grad_x * vel_y, axis=0)
    bend_xy = jnp.sum(grad_y * rot_y - grad_x * rot_x, axis=0)
    shear_xz = jnp.sum(grad_x * vel_z, axis=0) + 0.25 * jnp.sum(rot_y, axis=0)
    shear_yz = jnp.sum(grad_y * vel_z, axis=0) - 0.25 * jnp.sum(rot_x, axis=0)
    layers = []
    membrane = []
    moments = []
    for layer in range(5):
        height = 0.5 * thickness * LOBATTO_POINTS[layer]
        strain_xx = memb_xx + height * bend_xx
        strain_yy = memb_yy + height * bend_yy
        strain_xy = memb_xy + height * bend_xy
        trial_xx = old_stress[layer, 0] + PLANE_MODULUS * (strain_xx + POISSON * strain_yy)
        trial_yy = old_stress[layer, 1] + PLANE_MODULUS * (strain_yy + POISSON * strain_xx)
        trial_xy = old_stress[layer, 2] + PLANE_MODULUS * 0.5 * (1.0 - POISSON) * strain_xy
        trial_xz = old_stress[layer, 3] + SHEAR_MODULUS * shear_xz
        trial_yz = old_stress[layer, 4] + SHEAR_MODULUS * shear_yz
        mises = jnp.sqrt(
            0.25 * (trial_xx + trial_yy) ** 2
            + 0.75 * (trial_xx - trial_yy) ** 2
            + 3.0 * (trial_xy**2 + trial_xz**2 + trial_yz**2)
        )
        factor = yield_stress / jnp.maximum(mises, yield_stress)
        updated = jnp.stack([trial_xx, trial_yy, trial_xy, trial_xz, trial_yz]) * factor
        layers.append(updated)
        weight = LOBATTO_WEIGHTS[layer] * 0.5 * thickness * area
        membrane.append(weight * updated)
        moments.append(weight * height * updated[0:3])
    new_stress = jnp.stack(layers)
    force_sum = sum(membrane)
    moment_sum = sum(moments)
    force_x = grad_x * force_sum[0] + grad_y * force_sum[2]
    force_y = grad_y * force_sum[1] + grad_x * force_sum[2]
    force_z = grad_x * force_sum[3] + grad_y * force_sum[4]
    moment_x = -(grad_y * moment_sum[1] + grad_x * moment_sum[2]) - 0.25 * force_sum[4]
    moment_y = grad_x * moment_sum[0] + grad_y * moment_sum[2] + 0.25 * force_sum[3]
    return (jnp.stack([force_x, force_y, force_z, moment_x, moment_y]), new_stress)


def ranks_and_counts(target, number):
    total_rows = target.shape[0]
    rows = min(512, total_rows)
    blocks = total_rows // rows
    owners = jnp.arange(number, dtype=jnp.int32)
    onehot = (target.reshape(blocks, rows)[:, :, None] == owners[None, None, :]).astype(
        jnp.bfloat16
    )
    earlier = (jnp.arange(rows)[:, None] > jnp.arange(rows)[None, :]).astype(jnp.bfloat16)
    within = jnp.einsum("ij,bjd->bid", earlier, onehot, preferred_element_type=jnp.float32)
    totals = jnp.sum(onehot.astype(jnp.float32), axis=1)
    offsets = jnp.cumsum(totals, axis=0) - totals
    rank = jnp.sum((within + offsets[:, None, :]) * onehot.astype(jnp.float32), axis=2)
    counts = jnp.sum(totals, axis=0)
    return (rank.reshape(total_rows).astype(jnp.int32), counts.astype(jnp.int32))


def face_normals(face_angle):
    azimuth, elevation = (face_angle[0], face_angle[1])
    return jnp.stack(
        [
            jnp.cos(azimuth) * jnp.cos(elevation),
            jnp.sin(azimuth) * jnp.cos(elevation),
            jnp.sin(elevation),
        ]
    )


def pair_forces(node_block, face_block, live):
    offset = node_block[0:3, :, :, None] - face_block[0:3, :, None, :]
    normal = face_block[3:6, :, None, :]
    depth = jnp.maximum(-jnp.sum(normal * offset, axis=0), 0.0)
    reach = jnp.exp(-jnp.sum(offset * offset, axis=0) / REACH_SQ)
    along = jnp.sum(normal * node_block[3:6, :, :, None], axis=0)
    magnitude = face_block[6][:, None, :] * reach * depth * (1.0 - DAMPING * along)
    magnitude = magnitude * node_block[6][:, :, None] * live[:, None, None]
    return jnp.einsum("bij,cbj->cbi", magnitude, face_block[3:6], precision=lax.Precision.HIGHEST)


def body(
    velocity,
    position,
    inv_mass,
    connectivity,
    shape_grad,
    area,
    thickness,
    yield_stress,
    stress,
    contact_owner,
    face_center,
    face_angle,
    face_stiffness,
    ghost_list,
    pair_node,
    pair_face,
    pair_count,
):
    dom_count = lax.axis_size("dom")
    sub_count = lax.axis_size("sub")
    devices = dom_count * sub_count
    node_dev = velocity.shape[1]
    capacity = 2 * node_dev // devices
    padded = extended_2(velocity, ((("dom", "sub"), 1),), HALO)
    extent = padded.shape[1]
    rows = min(256, node_dev)
    blocks = node_dev // rows
    span = rows + 2 * HALO
    reach = 1 + (2 * HALO + rows - 1) // rows
    limit = max(1, 2**20 // (rows * span))
    group = math.gcd(blocks, 1 << limit.bit_length() - 1)
    turns = blocks // group
    extended = jnp.pad(padded, ((0, 0), (0, (blocks + reach) * rows - extent)))
    pieces = extended.reshape(5, blocks + reach, rows)
    windows = jnp.concatenate([pieces[:, shift : shift + blocks] for shift in range(reach)], axis=2)
    starts = (jnp.arange(blocks, dtype=jnp.int32) * rows)[None, :, None]
    local = connectivity.reshape(4, blocks, rows) - starts
    local_grouped = local.transpose(1, 0, 2).reshape(turns, group, 4, rows)
    window_grouped = windows.transpose(1, 0, 2).reshape(turns, group, 5, span)
    positions = jnp.arange(span, dtype=jnp.int32)

    def pick_corners(inputs):
        where, window = inputs
        selector = (where[..., None] == positions).astype(jnp.float32)
        return jnp.einsum("gaew,gcw->gcae", selector, window, precision=lax.Precision.HIGHEST)

    corners = lax.map(pick_corners, (local_grouped, window_grouped))
    corners = corners.transpose(2, 3, 0, 1, 4).reshape(5, 4, node_dev)
    forces, new_stress = element_forces(corners, shape_grad, area, thickness, yield_stress, stress)
    forces_grouped = forces.reshape(5, 4, turns, group, rows).transpose(2, 3, 0, 1, 4)

    def spread_forces(inputs):
        where, part = inputs
        selector = (where[..., None] == positions).astype(jnp.float32)
        return jnp.einsum("gaew,gcae->gcw", selector, part, precision=lax.Precision.HIGHEST)

    shares = lax.map(spread_forces, (local_grouped, forces_grouped))
    shares = shares.reshape(blocks, 5, span).transpose(1, 0, 2)
    shares = shares.reshape(5, blocks, reach, rows)
    gathered = jnp.zeros((5, blocks + reach, rows), jnp.float32)
    for shift in range(reach):
        gathered = gathered + jnp.pad(shares[:, :, shift], ((0, 0), (shift, reach - shift), (0, 0)))
    summed = gathered.reshape(5, (blocks + reach) * rows)[:, :extent]
    rims = jnp.concatenate([summed[:, :HALO], summed[:, HALO + node_dev :]], axis=1)
    arrived = extended_2(rims, ((("dom", "sub"), 1),), HALO)
    internal = summed[:, HALO : HALO + node_dev]
    internal = internal.at[:, :HALO].add(arrived[:, :HALO])
    internal = internal.at[:, node_dev - HALO :].add(arrived[:, 3 * HALO :])
    target = contact_owner[:, 0]
    ranks, sent_counts = ranks_and_counts(target, devices)
    slots = target * capacity + ranks
    payload = jnp.concatenate(
        [position, velocity[0:3], jnp.ones((1, node_dev), jnp.float32)], axis=0
    )
    outgoing = jnp.zeros((7, devices * capacity), jnp.float32).at[:, slots].set(payload)
    grouped = outgoing.reshape(7, dom_count, sub_count, capacity)
    incoming = one_exchange(grouped, ("dom", "sub"), ("dom", "sub"), (1, 2), (1, 2)).reshape(
        7, devices * capacity
    )
    face_data = jnp.concatenate(
        [face_center, face_normals(face_angle), face_stiffness[None, :]], axis=0
    )
    leaving = face_data[:, ghost_list]
    borrowed = extended_2(leaving, ((("dom", "sub"), 1),), GHOST)
    all_faces = jnp.concatenate([borrowed[:, :GHOST], face_data, borrowed[:, 3 * GHOST :]], axis=1)
    node_tiles = incoming.reshape(7, -1, TILE)
    face_tiles = all_faces.reshape(7, -1, TILE)
    tile_count = node_tiles.shape[1]
    pair_total = pair_node.shape[0]
    block = math.gcd(32, pair_total)
    tile_ids = jnp.arange(tile_count, dtype=jnp.int32)

    def one_block(step, accum):
        start = step * block
        node_ids = lax.dynamic_slice_in_dim(pair_node, start, block)
        face_ids = lax.dynamic_slice_in_dim(pair_face, start, block)
        live = (start + jnp.arange(block, dtype=jnp.int32) < pair_count[0]).astype(jnp.float32)
        result = pair_forces(
            jnp.take(node_tiles, node_ids, axis=1), jnp.take(face_tiles, face_ids, axis=1), live
        )
        onehot = (node_ids[:, None] == tile_ids[None, :]).astype(jnp.float32)
        return accum + jnp.einsum("cbi,bt->cti", result, onehot, precision=lax.Precision.HIGHEST)

    accum = lax.fori_loop(
        0, pair_total // block, one_block, jnp.zeros((3, tile_count, TILE), jnp.float32)
    )
    returned = accum.reshape(3, devices * capacity)
    grouped_back = returned.reshape(3, dom_count, sub_count, capacity)
    back = one_exchange(grouped_back, ("dom", "sub"), ("dom", "sub"), (1, 2), (1, 2)).reshape(
        3, devices * capacity
    )
    contact = back[:, slots]
    total = (-internal).at[0:3].add(contact)
    new_velocity = velocity + inv_mass[None, :] * total
    return (new_velocity, new_stress)


def solution(mesh):
    in_specs = (
        P(None, ("dom", "sub")),
        P(None, ("dom", "sub")),
        P(("dom", "sub")),
        P(None, ("dom", "sub")),
        P(None, None, ("dom", "sub")),
        P(("dom", "sub")),
        P(("dom", "sub")),
        P(("dom", "sub")),
        P(None, None, ("dom", "sub")),
        P(("dom", "sub"), None),
        P(None, ("dom", "sub")),
        P(None, ("dom", "sub")),
        P(("dom", "sub")),
        P(("dom", "sub")),
        P(("dom", "sub")),
        P(("dom", "sub")),
        P(("dom", "sub")),
    )
    out_specs = (P(None, ("dom", "sub")), P(None, None, ("dom", "sub")))
    return jax.shard_map(body, mesh=mesh, in_specs=in_specs, out_specs=out_specs, check_vma=False)
```

profile of v0, /device:TPU:1, one launch (start us, length us, event | category | flops | bytes accessed | tf_op | source)
XLA Modules:
  0.0 320.6 jit_solution(16983339858782647975)
XLA Ops:
  1.3 3.9 %collective-permute-start = (f32[5,128]{1,0:T(8,128)S(1)}, f32[5,128]{1,0:T(8,128)S(1)}, u32[]{:S(2)}, u32[]{:S(2)}) collective-permute-start(f32[5,128]{1,0:T(8,128)S(1)} %get-tuple-element.534), channel_id=1, source_target_pairs={{0,1},{1,2},{2,3},{3,4},{4,5},{5,6},{6,7},{7,8},{8,9},{9,10},{10,1... | collective-permute-start | bytes 7688 | tf_op jit(solution)/shard_map/ppermute | solution.py:30
  5.3 3.7 %collective-permute-start.1 = (f32[5,128]{1,0:T(8,128)S(1)}, f32[5,128]{1,0:T(8,128)S(1)}, u32[]{:S(2)}, u32[]{:S(2)}) collective-permute-start(f32[5,128]{1,0:T(8,128)S(1)} %get-tuple-element.535), channel_id=1, source_target_pairs={{1,0},{2,1},{3,2},{4,3},{5,4},{6,5},{7,6},{8,7},{9,8},{10,9},{11,1... | collective-permute-start | bytes 7688 | tf_op jit(solution)/shard_map/ppermute | solution.py:31
  9.0 1.3 slice_sine_fusion
  10.3 0.8 concatenate.59
  12.2 1.0 gather_fusion.2
  14.0 1.9 collective-permute-start.4
  15.9 4.9 %collective-permute-start.5 = (f32[7,256]{0,1:T(8,128)}, f32[7,256]{0,1:T(8,128)}, u32[]{:S(2)}, u32[]{:S(2)}) collective-permute-start(f32[7,256]{0,1:T(8,128)} %get-tuple-element.524), channel_id=1, source_target_pairs={{1,0},{2,1},{3,2},{4,3},{5,4},{6,5},{7,6},{8,7},{9,8},{10,9},{11,1... | collective-permute-start | bytes 21512 | tf_op jit(solution)/shard_map/ppermute | solution.py:31
  21.2 1.5 reduce.17
  23.3 1.9 fusion.52
  25.5 2.7 copy.194
  28.2 24.6 %scatter_custom_fusion = f32[7,16384]{0,1:T(8,128)} fusion(s32[8192]{0:T(1024)S(1)} %bitcast.408, f32[8192,7]{1,0:T(8,128)} %copy.194, f32[]{:T(128)} %constant.237.clone.1), kind=kCustom, calls=%fused_computation.79 | custom fusion | bytes 459264 | tf_op jit(solution)/shard_map/scatter | solution.py:224
  52.8 6.0 %copy.195 = f32[32,4,7,1,1,128]{5,4,3,2,1,0:T(1,128)} copy(f32[32,4,7,1,1,128]{2,5,1,0,4,3:T(8,128)} %bitcast.315) | data formatting | bytes 917504 | tf_op jit(solution)/shard_map/transpose;transpose | solution.py:56
  58.8 11.5 %all-to-all-start = ((f32[128,7,1,1,128]{4,3,2,1,0:T(1,128)}), f32[128,7,1,1,128]{4,3,2,1,0:T(1,128)S(1)}, u32[]{:S(2)}, u32[]{:S(2)}) async-start(f32[128,7,1,1,128]{4,3,2,1,0:T(1,128)} %bitcast.88), calls=%async_computation | async-start | bytes 917504 | tf_op jit(solution)/shard_map/all_to_all | solution.py:59
  71.8 2.7 copy.204
  75.4 37.3 %while.39 = (s32[]{:T(128)}, f32[4,8,5,4,256]{4,2,3,1,0:T(8,128)}, f32[4,8,5,512]{3,2,1,0:T(8,128)S(1)}, s32[4,8,4,256]{3,2,1,0:T(4,128)S(1)}, s32[]{:T(128)}) while((s32[]{:T(128)}, f32[4,8,5,4,256]{4,2,3,1,0:T(8,128)}, f32[4,8,5,512]{3,2,1,0:T(8,128)S(1)}, s32[4,8,4,256]{3,2,1,0:T(4,128)S(1)}, s32[]{:T(128)}) %tuple.248), condition=%wide.region_1.2_spmd.clone, body=%wide.region_0.1_spmd.clone.sunk | while | flops 255852544 | bytes 492609 | solution.py:196
  75.4 9.3 %fusion.101 = f32[4,8,5,4,256]{4,2,3,1,0:T(8,128)} fusion(f32[4,8,5,4,256]{4,2,3,1,0:T(8,128)} %get-tuple-element.681, s32[]{:T(128)} %get-tuple-element.680, s32[8,4,256]{2,1,0:T(4,128)S(1)} %dynamic-slice_bitcast_fusion.4, f32[4,8,5,512]{3,2,1,0:T(8,128)S(1)} %get-tuple-element.687), kind=kOutput, calls=%fused_computation.12.clone.1 | convolution fusion | flops 255852544 | bytes 427008 | tf_op jit(solution)/shard_map/while/body/eval_jaxpr/gaew,gcw->gcae/dot_general | solution.py:194
  84.7 9.3 %fusion.101 = f32[4,8,5,4,256]{4,2,3,1,0:T(8,128)} fusion(f32[4,8,5,4,256]{4,2,3,1,0:T(8,128)} %get-tuple-element.681, s32[]{:T(128)} %get-tuple-element.680, s32[8,4,256]{2,1,0:T(4,128)S(1)} %dynamic-slice_bitcast_fusion.4, f32[4,8,5,512]{3,2,1,0:T(8,128)S(1)} %get-tuple-element.687), kind=kOutput, calls=%fused_computation.12.clone.1 | convolution fusion | flops 255852544 | bytes 427008 | tf_op jit(solution)/shard_map/while/body/eval_jaxpr/gaew,gcw->gcae/dot_general | solution.py:194
  94.1 9.3 %fusion.101 = f32[4,8,5,4,256]{4,2,3,1,0:T(8,128)} fusion(f32[4,8,5,4,256]{4,2,3,1,0:T(8,128)} %get-tuple-element.681, s32[]{:T(128)} %get-tuple-element.680, s32[8,4,256]{2,1,0:T(4,128)S(1)} %dynamic-slice_bitcast_fusion.4, f32[4,8,5,512]{3,2,1,0:T(8,128)S(1)} %get-tuple-element.687), kind=kOutput, calls=%fused_computation.12.clone.1 | convolution fusion | flops 255852544 | bytes 427008 | tf_op jit(solution)/shard_map/while/body/eval_jaxpr/gaew,gcw->gcae/dot_general | solution.py:194
  103.4 9.3 %fusion.101 = f32[4,8,5,4,256]{4,2,3,1,0:T(8,128)} fusion(f32[4,8,5,4,256]{4,2,3,1,0:T(8,128)} %get-tuple-element.681, s32[]{:T(128)} %get-tuple-element.680, s32[8,4,256]{2,1,0:T(4,128)S(1)} %dynamic-slice_bitcast_fusion.4, f32[4,8,5,512]{3,2,1,0:T(8,128)S(1)} %get-tuple-element.687), kind=kOutput, calls=%fused_computation.12.clone.1 | convolution fusion | flops 255852544 | bytes 427008 | tf_op jit(solution)/shard_map/while/body/eval_jaxpr/gaew,gcw->gcae/dot_general | solution.py:194
  112.7 4.1 %slice_reduce_fusion = (f32[4,8,256]{2,1,0:T(8,128)S(1)}, f32[4,8,256]{2,1,0:T(8,128)S(1)}, f32[1,4,4,8,256]{4,0,1,3,2:T(1,128)S(1)}, f32[1,4,4,8,256]{4,0,1,3,2...) fusion(f32[5,4,4,8,256]{4,0,1,3,2:T(8,128)} %bitcast.343), kind=kLoop, calls=%fused_computation.233 | loop fusion | flops 49152 | bytes 1376256 | tf_op jit(solution)/shard_map/reduce_sum | solution.py:74
  119.0 0.9 bitcast_add_fusion
  120.7 1.1 slice_add_fusion.2
  121.8 1.2 slice_add_fusion.4
  123.1 0.8 maximum_divide_fusion.4
  125.0 0.8 maximum_divide_fusion.2
  125.9 0.9 maximum_divide_fusion
  126.7 1.0 stack.158
  127.7 1.5 multiply_multiply_fusion.7
  129.9 1.1 stack.146
  131.0 1.1 stack.142
  132.1 1.0 multiply_add_fusion.1
  133.9 26.4 %while.40 = (s32[]{:T(128)}, f32[4,8,5,512]{3,2,1,0:T(8,128)S(1)}, f32[4,8,5,4,256]{4,1,0,3,2:T(8,128)S(1)}, s32[4,8,4,256]{3,2,1,0:T(4,128)S(1)}, s32[]{:T(128)}) while((s32[]{:T(128)}, f32[4,8,5,512]{3,2,1,0:T(8,128)S(1)}, f32[4,8,5,4,256]{4,1,0,3,2:T(8,128)S(1)}, s32[4,8,4,256]{3,2,1,0:T(4,128)S(1)}, s32[]{:T(128)}) %tuple.249), condition=%wide.region_13.14_spmd.clone, body=%wide.region_12.13_spmd.clone.sunk | while | flops 255852544 | bytes 720969 | solution.py:206
  134.0 6.6 %fusion.102 = f32[4,8,5,512]{3,2,1,0:T(8,128)S(1)} fusion(f32[4,8,5,512]{3,2,1,0:T(8,128)S(1)} %get-tuple-element.696, s32[]{:T(128)} %get-tuple-element.695, s32[8,4,256]{2,1,0:T(4,128)S(1)} %dynamic-slice_bitcast_fusion.5, f32[1,8,5,4,256]{4,1,0,3,2:T(8,128)S(1)} %constant_dynamic-slice_fusion.2), kind=kOutput, calls=%fused_computation.21.clone.1 | convolution fusion | flops 255852544 | bytes 327684 | tf_op jit(solution)/shard_map/while/body/eval_jaxpr/gaew,gcae->gcw/dot_general | solution.py:204
  140.6 6.6 %fusion.102 = f32[4,8,5,512]{3,2,1,0:T(8,128)S(1)} fusion(f32[4,8,5,512]{3,2,1,0:T(8,128)S(1)} %get-tuple-element.696, s32[]{:T(128)} %get-tuple-element.695, s32[8,4,256]{2,1,0:T(4,128)S(1)} %dynamic-slice_bitcast_fusion.5, f32[1,8,5,4,256]{4,1,0,3,2:T(8,128)S(1)} %constant_dynamic-slice_fusion.2), kind=kOutput, calls=%fused_computation.21.clone.1 | convolution fusion | flops 255852544 | bytes 327684 | tf_op jit(solution)/shard_map/while/body/eval_jaxpr/gaew,gcae->gcw/dot_general | solution.py:204
  147.2 6.6 %fusion.102 = f32[4,8,5,512]{3,2,1,0:T(8,128)S(1)} fusion(f32[4,8,5,512]{3,2,1,0:T(8,128)S(1)} %get-tuple-element.696, s32[]{:T(128)} %get-tuple-element.695, s32[8,4,256]{2,1,0:T(4,128)S(1)} %dynamic-slice_bitcast_fusion.5, f32[1,8,5,4,256]{4,1,0,3,2:T(8,128)S(1)} %constant_dynamic-slice_fusion.2), kind=kOutput, calls=%fused_computation.21.clone.1 | convolution fusion | flops 255852544 | bytes 327684 | tf_op jit(solution)/shard_map/while/body/eval_jaxpr/gaew,gcae->gcw/dot_general | solution.py:204
  153.8 6.6 %fusion.102 = f32[4,8,5,512]{3,2,1,0:T(8,128)S(1)} fusion(f32[4,8,5,512]{3,2,1,0:T(8,128)S(1)} %get-tuple-element.696, s32[]{:T(128)} %get-tuple-element.695, s32[8,4,256]{2,1,0:T(4,128)S(1)} %dynamic-slice_bitcast_fusion.5, f32[1,8,5,4,256]{4,1,0,3,2:T(8,128)S(1)} %constant_dynamic-slice_fusion.2), kind=kOutput, calls=%fused_computation.21.clone.1 | convolution fusion | flops 255852544 | bytes 327684 | tf_op jit(solution)/shard_map/while/body/eval_jaxpr/gaew,gcae->gcw/dot_general | solution.py:204
  161.3 2.8 copy.190
  164.1 0.9 fusion.81
  164.9 3.3 %collective-permute-start.2 = (f32[5,128]{0,1:T(8,128)S(1)}, f32[5,128]{0,1:T(8,128)S(1)}, u32[]{:S(2)}, u32[]{:S(2)}) collective-permute-start(f32[5,128]{0,1:T(8,128)S(1)} %get-tuple-element.460), channel_id=1, source_target_pairs={{0,1},{1,2},{2,3},{3,4},{4,5},{5,6},{6,7},{7,8},{8,9},{9,10},{10,1... | collective-permute-start | bytes 7688 | tf_op jit(solution)/shard_map/ppermute | solution.py:30
  168.2 3.7 %collective-permute-start.3 = (f32[5,128]{0,1:T(8,128)S(1)}, f32[5,128]{0,1:T(8,128)S(1)}, u32[]{:S(2)}, u32[]{:S(2)}) collective-permute-start(f32[5,128]{0,1:T(8,128)S(1)} %get-tuple-element.459), channel_id=1, source_target_pairs={{1,0},{2,1},{3,2},{4,3},{5,4},{6,5},{7,6},{8,7},{9,8},{10,9},{11,1... | collective-permute-start | bytes 7688 | tf_op jit(solution)/shard_map/ppermute | solution.py:31
  176.0 4.4 %slice.395 = f32[5,8192]{0,1:T(8,128)} slice(f32[5,8704]{0,1:T(8,128)} %bitcast.317), slice={[0:5], [128:8320]} | slice | bytes 327680 | tf_op jit(solution)/shard_map/slice | solution.py:215
  180.4 2.1 fusion.75
  182.5 1.0 copy.192
  183.5 1.0 copy.193
  185.2 43.9 %while.41 = (s32[]{:T(128)}, f32[3,128,128]{2,1,0:T(8,128)S(1)}, s32[128]{0:T(128)S(1)}, s32[128]{0:T(128)S(1)}, f32[7,20,128]{2,0,1:T(8,128)S(1)}, /*index=5*/f...) while((s32[]{:T(128)}, f32[3,128,128]{2,1,0:T(8,128)S(1)}, ...), condition=%wide.region_23.24_spmd.clone, body=%wide.region_19.23_spmd.clone.sunk | while | flops 53115464 | bytes 15149361 | solution.py:253
  186.9 4.3 %fusion.109 = (f32[32,128,128]{2,1,0:T(8,128)S(1)}, f32[32,128,128]{2,1,0:T(8,128)S(1)}, f32[32,128,128]{2,1,0:T(8,128)S(1)}) fusion(f32[3,32,128]{2,1,0:T(8,128)S(1)} %copy.248, f32[3,32,128]{2,1,0:T(8,128)S(1)} %copy.249, f32[3,32,128]{2,1,0:T(8,128)S(1)} %copy.250, f32[3,32,128]{2,1,0:T(8,128)S(1)} %copy.251), kind=kLoop, calls=%fused_computation.27.clone.1 | loop fusion | flops 9437184 | bytes 6488064 | tf_op jit(solution)/shard_map/while/body/eval_jaxpr/reduce_sum | solution.py:142
  191.9 3.9 %fusion.110 = f32[3,32,128]{2,0,1:T(4,128)S(1)} fusion(f32[32,128,128]{2,1,0:T(8,128)S(1)} %get-tuple-element.672, f32[32,128,128]{2,1,0:T(8,128)S(1)} %get-tuple-element.673, f32[32,128,128]{2,1,0:T(8,128)S(1)} %get-tuple-element.674, f32[32]{0:T(128)S(1)} %compare_convert_fusion.2, f32[32,128]{1,0:T(8,128)S(1)} %bitcast.344, ...), kind=kOutput, calls=%fused_computation.45.clone.1 | convolution fusion | flops 24641536 | bytes 6439424 | tf_op jit(solution)/shard_map/while/body/eval_jaxpr/bij,cbj->cbi/dot_general | solution.py:146
  197.8 4.3 %fusion.109 = (f32[32,128,128]{2,1,0:T(8,128)S(1)}, f32[32,128,128]{2,1,0:T(8,128)S(1)}, f32[32,128,128]{2,1,0:T(8,128)S(1)}) fusion(f32[3,32,128]{2,1,0:T(8,128)S(1)} %copy.248, f32[3,32,128]{2,1,0:T(8,128)S(1)} %copy.249, f32[3,32,128]{2,1,0:T(8,128)S(1)} %copy.250, f32[3,32,128]{2,1,0:T(8,128)S(1)} %copy.251), kind=kLoop, calls=%fused_computation.27.clone.1 | loop fusion | flops 9437184 | bytes 6488064 | tf_op jit(solution)/shard_map/while/body/eval_jaxpr/reduce_sum | solution.py:142
  202.9 3.9 %fusion.110 = f32[3,32,128]{2,0,1:T(4,128)S(1)} fusion(f32[32,128,128]{2,1,0:T(8,128)S(1)} %get-tuple-element.672, f32[32,128,128]{2,1,0:T(8,128)S(1)} %get-tuple-element.673, f32[32,128,128]{2,1,0:T(8,128)S(1)} %get-tuple-element.674, f32[32]{0:T(128)S(1)} %compare_convert_fusion.2, f32[32,128]{1,0:T(8,128)S(1)} %bitcast.344, ...), kind=kOutput, calls=%fused_computation.45.clone.1 | convolution fusion | flops 24641536 | bytes 6439424 | tf_op jit(solution)/shard_map/while/body/eval_jaxpr/bij,cbj->cbi/dot_general | solution.py:146
  208.8 4.3 %fusion.109 = (f32[32,128,128]{2,1,0:T(8,128)S(1)}, f32[32,128,128]{2,1,0:T(8,128)S(1)}, f32[32,128,128]{2,1,0:T(8,128)S(1)}) fusion(f32[3,32,128]{2,1,0:T(8,128)S(1)} %copy.248, f32[3,32,128]{2,1,0:T(8,128)S(1)} %copy.249, f32[3,32,128]{2,1,0:T(8,128)S(1)} %copy.250, f32[3,32,128]{2,1,0:T(8,128)S(1)} %copy.251), kind=kLoop, calls=%fused_computation.27.clone.1 | loop fusion | flops 9437184 | bytes 6488064 | tf_op jit(solution)/shard_map/while/body/eval_jaxpr/reduce_sum | solution.py:142
  213.8 3.9 %fusion.110 = f32[3,32,128]{2,0,1:T(4,128)S(1)} fusion(f32[32,128,128]{2,1,0:T(8,128)S(1)} %get-tuple-element.672, f32[32,128,128]{2,1,0:T(8,128)S(1)} %get-tuple-element.673, f32[32,128,128]{2,1,0:T(8,128)S(1)} %get-tuple-element.674, f32[32]{0:T(128)S(1)} %compare_convert_fusion.2, f32[32,128]{1,0:T(8,128)S(1)} %bitcast.344, ...), kind=kOutput, calls=%fused_computation.45.clone.1 | convolution fusion | flops 24641536 | bytes 6439424 | tf_op jit(solution)/shard_map/while/body/eval_jaxpr/bij,cbj->cbi/dot_general | solution.py:146
  219.8 4.3 %fusion.109 = (f32[32,128,128]{2,1,0:T(8,128)S(1)}, f32[32,128,128]{2,1,0:T(8,128)S(1)}, f32[32,128,128]{2,1,0:T(8,128)S(1)}) fusion(f32[3,32,128]{2,1,0:T(8,128)S(1)} %copy.248, f32[3,32,128]{2,1,0:T(8,128)S(1)} %copy.249, f32[3,32,128]{2,1,0:T(8,128)S(1)} %copy.250, f32[3,32,128]{2,1,0:T(8,128)S(1)} %copy.251), kind=kLoop, calls=%fused_computation.27.clone.1 | loop fusion | flops 9437184 | bytes 6488064 | tf_op jit(solution)/shard_map/while/body/eval_jaxpr/reduce_sum | solution.py:142
  224.8 3.9 %fusion.110 = f32[3,32,128]{2,0,1:T(4,128)S(1)} fusion(f32[32,128,128]{2,1,0:T(8,128)S(1)} %get-tuple-element.672, f32[32,128,128]{2,1,0:T(8,128)S(1)} %get-tuple-element.673, f32[32,128,128]{2,1,0:T(8,128)S(1)} %get-tuple-element.674, f32[32]{0:T(128)S(1)} %compare_convert_fusion.2, f32[32,128]{1,0:T(8,128)S(1)} %bitcast.344, ...), kind=kOutput, calls=%fused_computation.45.clone.1 | convolution fusion | flops 24641536 | bytes 6439424 | tf_op jit(solution)/shard_map/while/body/eval_jaxpr/bij,cbj->cbi/dot_general | solution.py:146
  229.3 0.9 copy.202
  230.2 8.8 %all-to-all-start.1 = ((f32[128,3,1,1,128]{4,3,2,1,0:T(1,128)}), f32[128,3,1,1,128]{4,3,2,1,0:T(1,128)S(1)}, u32[]{:S(2)}, u32[]{:S(2)}) async-start(f32[128,3,1,1,128]{4,3,2,1,0:T(1,128)} %copy.202), calls=%async_computation.1 | async-start | bytes 393216 | tf_op jit(solution)/shard_map/all_to_all | solution.py:59
  239.0 1.5 fusion.76
  240.5 4.4 %neg.26 = f32[5,8192]{0,1:T(8,128)} negate(f32[5,8192]{0,1:T(8,128)} %fusion.76) | non-fusion elementwise | flops 40960 | bytes 327680 | tf_op jit(solution)/shard_map/neg | solution.py:262
  244.9 4.8 %all-to-all-done.1 = f32[128,3,1,1,128]{4,3,2,1,0:T(1,128)S(1)} async-done(((f32[128,3,1,1,128]{4,3,2,1,0:T(1,128)}), f32[128,3,1,1,128]{4,3,2,1,0:T(1,128)S(1)}, u32[]{:S(2)}, u32[]{:S(2)}) %all-to-all-start.1) | async-done | bytes 196640 | tf_op jit(solution)/shard_map/all_to_all | solution.py:59
  249.7 4.7 %copy.203 = f32[32,4,3,1,1,128]{2,5,1,0,4,3:T(8,128)} copy(f32[32,4,3,1,1,128]{5,4,3,2,1,0:T(1,128)S(1)} %bitcast.329) | data formatting | bytes 393216 | tf_op jit(solution)/shard_map/reshape | solution.py:60
  254.4 31.3 %gather_fusion.3 = f32[8192,3]{1,0:T(8,128)} fusion(f32[3,16384]{0,1:T(8,128)} %bitcast.319, s32[8192]{0:T(1024)S(1)} %copy-done.25), kind=kCustom, calls=%fused_computation.3 | custom fusion | bytes 229376 | tf_op jit(solution)/shard_map/gather | solution.py:261
  285.7 5.8 %slice_add_fusion = f32[3,8192]{0,1:T(8,128)} fusion(f32[5,8192]{0,1:T(8,128)} %neg.26, f32[8192,3]{1,0:T(8,128)} %gather_fusion.3), kind=kLoop, calls=%fused_computation.74 | loop fusion | flops 24576 | bytes 294912 | tf_op jit(solution)/shard_map/add | solution.py:262
  291.5 20.1 %scatter-add.14 = f32[5,8192]{0,1:T(8,128)} dynamic-update-slice(f32[5,8192]{0,1:T(8,128)} %neg.26, f32[3,8192]{0,1:T(8,128)} %slice_add_fusion, s32[]{:T(128)} %constant.236.clone.1, s32[]{:T(128)} %constant.236.clone.1) | dynamic-update-slice | bytes 196612 | tf_op jit(solution)/shard_map/scatter-add | solution.py:262
  311.6 5.4 %multiply_add_fusion = f32[5,8192]{0,1:T(8,128)} fusion(f32[5,8192]{0,1:T(8,128)} %copy.204, f32[5,8192]{0,1:T(8,128)} %scatter-add.14, f32[8192]{0:T(1024)S(1)} %copy-done.42), kind=kLoop, calls=%fused_computation.75 | loop fusion | flops 81920 | bytes 524288 | tf_op jit(solution)/shard_map/add | solution.py:263
  317.1 3.5 %copy.205 = f32[5,8192]{1,0:T(8,128)} copy(f32[5,8192]{0,1:T(8,128)} %multiply_add_fusion) | data formatting | bytes 327680
  (266 shorter events, 27.5 us)
Async XLA Ops:
  1.3 73.9 %collective-permute-start = (f32[5,128]{1,0:T(8,128)S(1)}, f32[5,128]{1,0:T(8,128)S(1)}, u32[]{:S(2)}, u32[]{:S(2)}) collective-permute-start(f32[5,128]{1,0:T(8,128)S(1)} %get-tuple-element.534), channel_id=1, source_target_pairs={{0,1},{1,2},{2,3},{3,4},{4,5},{5,6},{6,7},{7,8},{8,9},{9,10},{10,1... | collective-permute-start | bytes 7688 | tf_op jit(solution)/shard_map/ppermute | solution.py:30
  5.3 69.9 %collective-permute-start.1 = (f32[5,128]{1,0:T(8,128)S(1)}, f32[5,128]{1,0:T(8,128)S(1)}, u32[]{:S(2)}, u32[]{:S(2)}) collective-permute-start(f32[5,128]{1,0:T(8,128)S(1)} %get-tuple-element.535), channel_id=1, source_target_pairs={{1,0},{2,1},{3,2},{4,3},{5,4},{6,5},{7,6},{8,7},{9,8},{10,9},{11,1... | collective-permute-start | bytes 7688 | tf_op jit(solution)/shard_map/ppermute | solution.py:31
  14.0 168.5 %collective-permute-start.4 = (f32[7,256]{0,1:T(8,128)}, f32[7,256]{0,1:T(8,128)}, u32[]{:S(2)}, u32[]{:S(2)}) collective-permute-start(f32[7,256]{0,1:T(8,128)} %get-tuple-element.523), channel_id=1, source_target_pairs={{0,1},{1,2},{2,3},{3,4},{4,5},{5,6},{6,7},{7,8},{8,9},{9,10},{10,1... | collective-permute-start | bytes 21512 | tf_op jit(solution)/shard_map/ppermute | solution.py:30
  15.9 167.6 %collective-permute-start.5 = (f32[7,256]{0,1:T(8,128)}, f32[7,256]{0,1:T(8,128)}, u32[]{:S(2)}, u32[]{:S(2)}) collective-permute-start(f32[7,256]{0,1:T(8,128)} %get-tuple-element.524), channel_id=1, source_target_pairs={{1,0},{2,1},{3,2},{4,3},{5,4},{6,5},{7,6},{8,7},{9,8},{10,9},{11,1... | collective-permute-start | bytes 21512 | tf_op jit(solution)/shard_map/ppermute | solution.py:31
  23.3 2.0 copy-start.24
  23.3 2.1 slice-start
  23.3 2.1 copy-start.23
  52.8 17.6 %copy-start.2 = (f32[5,5,8192]{2,1,0:T(8,128)S(1)}, f32[5,5,8192]{2,1,0:T(8,128)}, u32[]{:S(2)}) copy-start(f32[5,5,8192]{2,1,0:T(8,128)} %param.37) | copy-start | bytes 2457604
  52.8 18.3 %copy-start.26 = (s32[4,8192]{1,0:T(4,128)S(1)}, s32[4,8192]{1,0:T(4,128)}, u32[]{:S(2)}) copy-start(s32[4,8192]{1,0:T(4,128)} %param.32) | copy-start | bytes 393220
  52.8 19.0 %copy-start.1 = (f32[5,8192]{1,0:T(8,128)S(1)}, f32[5,8192]{1,0:T(8,128)}, u32[]{:S(2)}) copy-start(f32[5,8192]{1,0:T(8,128)} %param.29) | copy-start | bytes 491524
  58.8 125.6 %all-to-all-start = ((f32[128,7,1,1,128]{4,3,2,1,0:T(1,128)}), f32[128,7,1,1,128]{4,3,2,1,0:T(1,128)S(1)}, u32[]{:S(2)}, u32[]{:S(2)}) async-start(f32[128,7,1,1,128]{4,3,2,1,0:T(1,128)} %bitcast.88), calls=%async_computation | async-start | bytes 917504 | tf_op jit(solution)/shard_map/all_to_all | solution.py:59
  112.7 4.9 %copy-start = (f32[2,4,8192]{2,1,0:T(4,128)S(1)}, f32[2,4,8192]{2,1,0:T(4,128)}, u32[]{:S(2)}) copy-start(f32[2,4,8192]{2,1,0:T(4,128)} %param.33) | copy-start | bytes 786436
  112.7 10.4 %copy-start.3 = (f32[8192]{0:T(1024)S(1)}, f32[8192]{0:T(1024)}, u32[]{:S(2)}) copy-start(f32[8192]{0:T(1024)} %param.35) | copy-start | bytes 98308
  112.7 10.4 %copy-start.4 = (f32[8192]{0:T(1024)S(1)}, f32[8192]{0:T(1024)}, u32[]{:S(2)}) copy-start(f32[8192]{0:T(1024)} %param.36) | copy-start | bytes 98308
  123.1 6.2 %copy-start.36 = (f32[1,8192]{1,0:T(1,128)S(1)}, f32[1,8192]{1,0:T(1,128)}, u32[]{:S(2)}) copy-start(f32[1,8192]{1,0:T(1,128)} %get-tuple-element.474) | copy-start | bytes 98308
  123.1 6.5 %copy-start.35 = (f32[1,8192]{1,0:T(1,128)S(1)}, f32[1,8192]{1,0:T(1,128)}, u32[]{:S(2)}) copy-start(f32[1,8192]{1,0:T(1,128)} %get-tuple-element.475) | copy-start | bytes 98308
  123.9 5.9 %copy-start.21 = (f32[8192]{0:T(1024)}, f32[8192]{0:T(1024)S(1)}, u32[]{:S(2)}) copy-start(f32[8192]{0:T(1024)S(1)} %get-tuple-element.429) | copy-start | bytes 98308
  123.9 5.9 %copy-start.22 = (f32[8192]{0:T(1024)}, f32[8192]{0:T(1024)S(1)}, u32[]{:S(2)}) copy-start(f32[8192]{0:T(1024)S(1)} %get-tuple-element.430) | copy-start | bytes 98308
  123.9 7.0 %copy-start.20 = (f32[8192]{0:T(1024)}, f32[8192]{0:T(1024)S(1)}, u32[]{:S(2)}) copy-start(f32[8192]{0:T(1024)S(1)} %get-tuple-element.428) | copy-start | bytes 98308
  125.0 5.9 %copy-start.6 = (f32[8192]{0:T(1024)}, f32[8192]{0:T(1024)S(1)}, u32[]{:S(2)}) copy-start(f32[8192]{0:T(1024)S(1)} %get-tuple-element.440) | copy-start | bytes 98308
  125.9 5.1 %copy-start.8 = (f32[8192]{0:T(1024)}, f32[8192]{0:T(1024)S(1)}, u32[]{:S(2)}) copy-start(f32[8192]{0:T(1024)S(1)} %get-tuple-element.442) | copy-start | bytes 98308
  125.9 5.1 %copy-start.10 = (f32[8192]{0:T(1024)}, f32[8192]{0:T(1024)S(1)}, u32[]{:S(2)}) copy-start(f32[8192]{0:T(1024)S(1)} %get-tuple-element.443) | copy-start | bytes 98308
  125.9 5.1 %copy-start.12 = (f32[8192]{0:T(1024)}, f32[8192]{0:T(1024)S(1)}, u32[]{:S(2)}) copy-start(f32[8192]{0:T(1024)S(1)} %get-tuple-element.444) | copy-start | bytes 98308
  129.2 1.7 copy-start.14
  129.3 1.7 copy-start.16
  129.3 1.7 copy-start.18
  129.3 4.0 %copy-start.37 = (f32[8192]{0:T(1024)S(1)}, f32[8192]{0:T(1024)}, u32[]{:S(2)}) copy-start(f32[8192]{0:T(1024)} %get-tuple-element.539) | copy-start | bytes 98308
  129.3 4.0 %copy-start.38 = (f32[8192]{0:T(1024)S(1)}, f32[8192]{0:T(1024)}, u32[]{:S(2)}) copy-start(f32[8192]{0:T(1024)} %get-tuple-element.540) | copy-start | bytes 98308
  129.3 4.0 %copy-start.39 = (f32[8192]{0:T(1024)S(1)}, f32[8192]{0:T(1024)}, u32[]{:S(2)}) copy-start(f32[8192]{0:T(1024)} %get-tuple-element.541) | copy-start | bytes 98308
  129.3 4.0 %copy-start.40 = (f32[8192]{0:T(1024)S(1)}, f32[8192]{0:T(1024)}, u32[]{:S(2)}) copy-start(f32[8192]{0:T(1024)} %get-tuple-element.542) | copy-start | bytes 98308
  129.3 4.0 %copy-start.41 = (f32[8192]{0:T(1024)S(1)}, f32[8192]{0:T(1024)}, u32[]{:S(2)}) copy-start(f32[8192]{0:T(1024)} %get-tuple-element.543) | copy-start | bytes 98308
  129.9 4.1 %copy-start.5 = (f32[4,8,5,512]{3,2,1,0:T(8,128)S(1)}, f32[4,8,5,512]{3,2,1,0:T(8,128)}, u32[]{:S(2)}) copy-start(f32[4,8,5,512]{3,2,1,0:T(8,128)} %custom-call.12) | copy-start | bytes 983044
  160.4 11.6 %copy-start.7 = (f32[8192]{0:T(1024)S(1)}, f32[8192]{0:T(1024)}, u32[]{:S(2)}) copy-start(f32[8192]{0:T(1024)} %copy-done.6) | copy-start | bytes 98308
  160.4 11.6 %copy-start.33 = (f32[1,1,8192]{2,1,0:T(1,128)S(1)}, f32[1,1,8192]{2,1,0:T(1,128)}, u32[]{:S(2)}) copy-start(f32[1,1,8192]{2,1,0:T(1,128)} %get-tuple-element.463) | copy-start | bytes 98308
  160.4 11.6 %copy-start.34 = (f32[1,1,8192]{2,1,0:T(1,128)S(1)}, f32[1,1,8192]{2,1,0:T(1,128)}, u32[]{:S(2)}) copy-start(f32[1,1,8192]{2,1,0:T(1,128)} %get-tuple-element.478) | copy-start | bytes 98308
  160.6 12.4 %copy-start.9 = (f32[8192]{0:T(1024)S(1)}, f32[8192]{0:T(1024)}, u32[]{:S(2)}) copy-start(f32[8192]{0:T(1024)} %copy-done.8) | copy-start | bytes 98308
  160.6 12.4 %copy-start.11 = (f32[8192]{0:T(1024)S(1)}, f32[8192]{0:T(1024)}, u32[]{:S(2)}) copy-start(f32[8192]{0:T(1024)} %copy-done.10) | copy-start | bytes 98308
  160.6 12.4 %copy-start.13 = (f32[8192]{0:T(1024)S(1)}, f32[8192]{0:T(1024)}, u32[]{:S(2)}) copy-start(f32[8192]{0:T(1024)} %copy-done.12) | copy-start | bytes 98308
  160.6 12.4 %copy-start.31 = (f32[1,1,8192]{2,1,0:T(1,128)S(1)}, f32[1,1,8192]{2,1,0:T(1,128)}, u32[]{:S(2)}) copy-start(f32[1,1,8192]{2,1,0:T(1,128)} %get-tuple-element.462) | copy-start | bytes 98308
  160.6 12.4 %copy-start.32 = (f32[1,1,8192]{2,1,0:T(1,128)S(1)}, f32[1,1,8192]{2,1,0:T(1,128)}, u32[]{:S(2)}) copy-start(f32[1,1,8192]{2,1,0:T(1,128)} %get-tuple-element.479) | copy-start | bytes 98308
  161.1 12.9 %copy-start.15 = (f32[8192]{0:T(1024)S(1)}, f32[8192]{0:T(1024)}, u32[]{:S(2)}) copy-start(f32[8192]{0:T(1024)} %copy-done.14) | copy-start | bytes 98308
  161.1 12.9 %copy-start.17 = (f32[8192]{0:T(1024)S(1)}, f32[8192]{0:T(1024)}, u32[]{:S(2)}) copy-start(f32[8192]{0:T(1024)} %copy-done.16) | copy-start | bytes 98308
  161.1 12.9 %copy-start.19 = (f32[8192]{0:T(1024)S(1)}, f32[8192]{0:T(1024)}, u32[]{:S(2)}) copy-start(f32[8192]{0:T(1024)} %copy-done.18) | copy-start | bytes 98308
  161.1 12.9 %copy-start.29 = (f32[1,1,8192]{2,1,0:T(1,128)S(1)}, f32[1,1,8192]{2,1,0:T(1,128)}, u32[]{:S(2)}) copy-start(f32[1,1,8192]{2,1,0:T(1,128)} %get-tuple-element.461) | copy-start | bytes 98308
  161.2 12.8 %copy-start.30 = (f32[1,1,8192]{2,1,0:T(1,128)S(1)}, f32[1,1,8192]{2,1,0:T(1,128)}, u32[]{:S(2)}) copy-start(f32[1,1,8192]{2,1,0:T(1,128)} %get-tuple-element.480) | copy-start | bytes 98308
  161.2 13.8 %copy-start.27 = (f32[1,1,8192]{2,1,0:T(1,128)S(1)}, f32[1,1,8192]{2,1,0:T(1,128)}, u32[]{:S(2)}) copy-start(f32[1,1,8192]{2,1,0:T(1,128)} %get-tuple-element.417) | copy-start | bytes 98308
  161.2 13.8 %copy-start.28 = (f32[1,1,8192]{2,1,0:T(1,128)S(1)}, f32[1,1,8192]{2,1,0:T(1,128)}, u32[]{:S(2)}) copy-start(f32[1,1,8192]{2,1,0:T(1,128)} %get-tuple-element.490) | copy-start | bytes 98308
  164.9 15.5 %collective-permute-start.2 = (f32[5,128]{0,1:T(8,128)S(1)}, f32[5,128]{0,1:T(8,128)S(1)}, u32[]{:S(2)}, u32[]{:S(2)}) collective-permute-start(f32[5,128]{0,1:T(8,128)S(1)} %get-tuple-element.460), channel_id=1, source_target_pairs={{0,1},{1,2},{2,3},{3,4},{4,5},{5,6},{6,7},{7,8},{8,9},{9,10},{10,1... | collective-permute-start | bytes 7688 | tf_op jit(solution)/shard_map/ppermute | solution.py:30
  168.2 70.8 %collective-permute-start.3 = (f32[5,128]{0,1:T(8,128)S(1)}, f32[5,128]{0,1:T(8,128)S(1)}, u32[]{:S(2)}, u32[]{:S(2)}) collective-permute-start(f32[5,128]{0,1:T(8,128)S(1)} %get-tuple-element.459), channel_id=1, source_target_pairs={{1,0},{2,1},{3,2},{4,3},{5,4},{6,5},{7,6},{8,7},{9,8},{10,9},{11,1... | collective-permute-start | bytes 7688 | tf_op jit(solution)/shard_map/ppermute | solution.py:31
  180.4 4.8 %copy-start.43 = (s32[128]{0:T(128)S(1)}, s32[128]{0:T(128)}, u32[]{:S(2)}) copy-start(s32[128]{0:T(128)} %param.43) | copy-start | bytes 1540
  180.4 4.8 %copy-start.44 = (s32[128]{0:T(128)S(1)}, s32[128]{0:T(128)}, u32[]{:S(2)}) copy-start(s32[128]{0:T(128)} %param.44) | copy-start | bytes 1540
  230.2 19.6 %all-to-all-start.1 = ((f32[128,3,1,1,128]{4,3,2,1,0:T(1,128)}), f32[128,3,1,1,128]{4,3,2,1,0:T(1,128)S(1)}, u32[]{:S(2)}, u32[]{:S(2)}) async-start(f32[128,3,1,1,128]{4,3,2,1,0:T(1,128)} %copy.202), calls=%async_computation.1 | async-start | bytes 393216 | tf_op jit(solution)/shard_map/all_to_all | solution.py:59
  249.7 4.7 %copy-start.25 = (s32[8192]{0:T(1024)S(1)}, s32[8192]{0:T(1024)}, u32[]{:S(2)}) copy-start(s32[8192]{0:T(1024)} %broadcast_clamp_fusion) | copy-start | bytes 98308
  291.5 20.1 %copy-start.42 = (f32[8192]{0:T(1024)S(1)}, f32[8192]{0:T(1024)}, u32[]{:S(2)}) copy-start(f32[8192]{0:T(1024)} %param.31) | copy-start | bytes 98308
where the time goes:
time: 323 us; the launch traced here: 321 us
  local copies, waits for them, and re-layouts  124 us (38%)
  matrix products  82.5 us (26%)
  other arithmetic  64.8 us (20%)
  starting transfers between devices  41.8 us (13%)
  waiting for transfers between devices  4.84 us (1%)
    dot_general x4, matrix products, pick_corners(): jnp.einsum('gaew,gcw->gcae', selector, window, precision=lax.Precision.HI...  37.3 us
    gather x1, local copies, waits for them, and re-layouts, body(): contact = back[:, slots]  31.3 us
    dot_general x4, matrix products, spread_forces(): jnp.einsum('gaew,gcae->gcw', selector, part, precision=lax.Precision.HIGH...  26.2 us
    scatter x1, local copies, waits for them, and re-layouts, body(): jnp.zeros((7, devices * capacity), jnp.float32).at[:, slots].set(payload)  24.6 us
    all_to_all x2, starting transfers between devices, one_exchange(): lax.all_to_all(blocks, axis, split_axis=0, concat_axis=0, tiled=True)  20.3 us
    scatter-add x1, local copies, waits for them, and re-layouts, body(): total = (-internal).at[0:3].add(contact)  20.1 us
    reduce_sum x4, other arithmetic, pair_forces(): reach = jnp.exp(-jnp.sum(offset * offset, axis=0) / REACH_SQ)  17.3 us
    dot_general x4, matrix products, pair_forces(): jnp.einsum('bij,cbj->cbi', magnitude, face_block[3:6], precision=lax.Prec...  15.5 us
  transfers between devices with their start and end apart: 8, of which 1 were waited for; matrix products, arithmetic and copies ran while one was open for 62% of the time, Pallas kernels for 0%

commit v1 on v0

v1 whole, which is shorter than its diff:
```python
import functools

import jax
import jax.numpy as jnp
from jax import lax
from jax.experimental import pallas as pl
from jax.experimental.pallas import tpu as pltpu
from jax.sharding import PartitionSpec as P

TILE = 128
HALO = 128
GHOST = 256
NODE_DEV = 8192
ROWS = NODE_DEV // 128
FACE_DEV = 2048
FACE_TILES = 20
DEVICES = 128
PAIRS = 128
EXT = ROWS + 8

LOBATTO_POINTS = (-1.0, -0.6546536707079771, 0.0, 0.6546536707079771, 1.0)
LOBATTO_WEIGHTS = (0.1, 49.0 / 90.0, 32.0 / 45.0, 49.0 / 90.0, 0.1)
PLANE_MODULUS = 1.0 / 0.91
POISSON = 0.3
SHEAR_MODULUS = 5.0 / 6.0 / 2.6
DAMPING = 0.3
REACH_SQ = 0.5
LOG2E = 1.4426950408889634

BF = jnp.bfloat16
F32 = jnp.float32
NT = (((1,), (1,)), ((), ()))
NN = (((1,), (0,)), ((), ()))


def dot(a, b, dims):
    return lax.dot_general(a, b, dims, preferred_element_type=F32)


def onehot(count, row):
    where = lax.broadcasted_iota(jnp.int32, (count, row.shape[1]), 0)
    return jnp.where(where == row, 1.0, 0.0).astype(BF)


def split(x, parts):
    out = []
    for _ in range(parts - 1):
        head = x.astype(BF)
        out.append(head)
        x = x - head.astype(F32)
    out.append(x.astype(BF))
    return out


def lane_aligned(x, size):
    return pl.ds(pl.multiple_of(x * size, size), size)


NODE_PARTS = 3


def slots_kernel(owner_ref, pos_ref, vel_ref, rank_ref, out_ref, run, acc, tri):
    later = lax.broadcasted_iota(jnp.int32, (256, 384), 0)
    column = lax.broadcasted_iota(jnp.int32, (256, 384), 1)
    tri[...] = jnp.where((later < column) | (column >= 256), 1.0, 0.0).astype(BF)
    run[...] = jnp.zeros_like(run)

    def rank_block(b):
        at = lane_aligned(b, 256)
        own = owner_ref[0:1, at]
        where = lax.broadcasted_iota(jnp.int32, (DEVICES, 256), 0)
        hot = jnp.where(where == own, 1.0, 0.0)
        counts = dot(hot.astype(BF), tri[...], NN)
        base = run[...]
        seen = counts[:, :256] + jnp.concatenate([base, base], axis=1)
        rank_ref[0:1, at] = jnp.sum(hot * seen, axis=0, keepdims=True)
        run[...] = base + counts[:, 256:]

    def rank_step(b, _):
        rank_block(2 * b)
        rank_block(2 * b + 1)
        return 0

    lax.fori_loop(0, NODE_DEV // 512, rank_step, 0)
    acc[...] = jnp.zeros_like(acc)

    def place(b, _):
        at = lane_aligned(b, 1024)
        own = owner_ref[0:1, at]
        column = (own & 1) * 128 + rank_ref[0:1, at].astype(jnp.int32)
        hot = onehot(256, column)
        group = onehot(64, own // 2)
        rows = []
        for c in range(6):
            value = pos_ref[c : c + 1, at] if c < 3 else vel_ref[c - 3 : c - 2, at]
            rows += [group * part for part in split(value, NODE_PARTS)]
        rows.append(group)
        placed = dot(jnp.concatenate(rows, axis=0), hot, NT)
        for c in range(6):
            first = c * NODE_PARTS * 64
            total = placed[first : first + 64]
            for part in range(1, NODE_PARTS):
                total = total + placed[first + part * 64 : first + part * 64 + 64]
            acc[c * 64 : c * 64 + 64, :] += total
        acc[384:448, :] += placed[6 * NODE_PARTS * 64 :]
        return 0

    lax.fori_loop(0, NODE_DEV // 1024, place, 0)
    for first in range(0, 64, 8):
        for low in range(2):
            for c in range(8):
                rows = pl.ds(first * 16 + low * 8 + c, 8, stride=16)
                if c < 7:
                    part = acc[c * 64 + first : c * 64 + first + 8, low * 128 : low * 128 + 128]
                else:
                    part = jnp.zeros((8, 128), F32)
                out_ref[rows, :] = part


def slots(owner, position, velocity):
    return pl.pallas_call(
        slots_kernel,
        out_shape=(
            jax.ShapeDtypeStruct((1, NODE_DEV), F32),
            jax.ShapeDtypeStruct((DEVICES * 8, 128), F32),
        ),
        scratch_shapes=[
            pltpu.VMEM((DEVICES, 128), F32),
            pltpu.VMEM((448, 256), F32),
            pltpu.VMEM((256, 384), BF),
        ],
        compiler_params=pltpu.CompilerParams(vmem_limit_bytes=40 * 2**20),
        name="slots",
    )(owner, position, velocity)


def lend_kernel(list_ref, face_ref, out_ref):
    for g in range(4):
        index = jnp.broadcast_to(list_ref[:, 128 * g : 128 * g + 128], (8, 128))
        low, high = index & 127, index >> 7
        found = jnp.zeros((8, 128), F32)
        for t in range(FACE_DEV // 128):
            part = jnp.take_along_axis(face_ref[:, 128 * t : 128 * t + 128], low, axis=1)
            found = jnp.where(high == t, part, found)
        out_ref[:, 128 * g : 128 * g + 128] = found


def lend(ghost_list, faces):
    return pl.pallas_call(
        lend_kernel,
        out_shape=jax.ShapeDtypeStruct((8, 2 * GHOST), F32),
        name="lend",
    )(ghost_list, faces)


def constitutive(corner, grad_x, grad_y, area, thickness, limit, old):
    def over(f):
        total = f(0)
        for a in range(1, 4):
            total = total + f(a)
        return total

    vx, vy, vz, rx, ry = corner
    memb_xx = over(lambda a: grad_x[a] * vx[a])
    bend_xx = over(lambda a: grad_x[a] * ry[a])
    memb_yy = over(lambda a: grad_y[a] * vy[a])
    bend_yy = -over(lambda a: grad_y[a] * rx[a])
    memb_xy = over(lambda a: grad_y[a] * vx[a] + grad_x[a] * vy[a])
    bend_xy = over(lambda a: grad_y[a] * ry[a] - grad_x[a] * rx[a])
    shear_xz = over(lambda a: grad_x[a] * vz[a]) + 0.25 * over(lambda a: ry[a])
    shear_yz = over(lambda a: grad_y[a] * vz[a]) - 0.25 * over(lambda a: rx[a])
    add_xz, add_yz = SHEAR_MODULUS * shear_xz, SHEAR_MODULUS * shear_yz
    half = 0.5 * thickness
    volume = half * area
    new, force, moment = [], [0.0] * 5, [0.0] * 3
    for layer in range(5):
        height = half * LOBATTO_POINTS[layer]
        exx = memb_xx + height * bend_xx
        eyy = memb_yy + height * bend_yy
        exy = memb_xy + height * bend_xy
        t0 = old(layer, 0) + PLANE_MODULUS * (exx + POISSON * eyy)
        t1 = old(layer, 1) + PLANE_MODULUS * (eyy + POISSON * exx)
        t2 = old(layer, 2) + PLANE_MODULUS * 0.5 * (1.0 - POISSON) * exy
        t3 = old(layer, 3) + add_xz
        t4 = old(layer, 4) + add_yz
        plus, minus = t0 + t1, t0 - t1
        mises = jnp.sqrt(
            0.25 * (plus * plus) + 0.75 * (minus * minus) + 3.0 * (t2 * t2 + t3 * t3 + t4 * t4)
        )
        factor = limit / jnp.maximum(mises, limit)
        updated = [t * factor for t in (t0, t1, t2, t3, t4)]
        new.append(updated)
        weight = LOBATTO_WEIGHTS[layer] * volume
        weighted = [weight * u for u in updated]
        force = [f + w for f, w in zip(force, weighted)]
        moment = [m + height * w for m, w in zip(moment, weighted)]
    corners = []
    for a in range(4):
        gx, gy = grad_x[a], grad_y[a]
        corners.append(
            [
                gx * force[0] + gy * force[2],
                gy * force[1] + gx * force[2],
                gx * force[3] + gy * force[4],
                -(gy * moment[1] + gx * moment[2]) - 0.25 * force[4],
                gx * moment[0] + gy * moment[2] + 0.25 * force[3],
            ]
        )
    return new, corners


def elements_kernel(
    vel_ref, low_ref, high_ref, conn_ref, grad_ref, area_ref, thick_ref, limit_ref, stress_ref,
    new_ref, sum_ref, vel, conn, grad, stress, spread,
):
    vel[pl.ds(0, 5, stride=EXT), :] = low_ref[...]
    vel[pl.ds(ROWS + 1, 5, stride=EXT), :] = high_ref[...]

    def unpack(j, _):
        at = lane_aligned(j, 128)
        vel[pl.ds(j + 1, 5, stride=EXT), :] = vel_ref[:, at]
        conn[pl.ds(j, 4, stride=ROWS), :] = conn_ref[:, at] - 128 * j
        for axis in range(2):
            grad[pl.ds(axis * 4 * ROWS + j, 4, stride=ROWS), :] = grad_ref[axis, :, at]
        for layer in range(5):
            stress[pl.ds(layer * 5 * ROWS + j, 5, stride=ROWS), :] = stress_ref[layer, :, at]
        return 0

    lax.fori_loop(0, ROWS, unpack, 0, unroll=8)
    spread[...] = jnp.zeros_like(spread)

    def group(g, _):
        def rows(field):
            return pl.ds(pl.multiple_of(field * ROWS + 8 * g, 8), 8)

        here = pl.ds(pl.multiple_of(8 * g, 8), 8)
        index = [conn[rows(a), :] for a in range(4)]
        low = [i & 127 for i in index]
        part_of = [i >> 7 for i in index]
        corner = []
        for c in range(5):
            window = [vel[pl.ds(c * EXT + 8 * g + k, 8), :] for k in range(3)]
            values = []
            for a in range(4):
                got = [jnp.take_along_axis(w, low[a], axis=1) for w in window]
                values.append(
                    jnp.where(part_of[a] == 0, got[0], jnp.where(part_of[a] == 1, got[1], got[2]))
                )
            corner.append(values)
        grad_x = [grad[rows(a), :] for a in range(4)]
        grad_y = [grad[rows(4 + a), :] for a in range(4)]
        new, forces = constitutive(
            corner, grad_x, grad_y, area_ref[here, :], thick_ref[here, :], limit_ref[here, :],
            lambda layer, c: stress[rows(5 * layer + c), :],
        )
        for layer in range(5):
            for c in range(5):
                stress[rows(5 * layer + c), :] = new[layer][c]
        for a in range(4):
            for c in range(5):
                spread[a, pl.ds(64 * g + c, 8, stride=8), :] = forces[a][c]
        return 0

    lax.fori_loop(0, 8, group, 0)

    def pack(j, _):
        at = lane_aligned(j, 128)
        for layer in range(5):
            new_ref[layer, :, at] = stress[pl.ds(layer * 5 * ROWS + j, 5, stride=ROWS), :]
        return 0

    lax.fori_loop(0, ROWS, pack, 0, unroll=8)
    sum_ref[...] = jnp.zeros_like(sum_ref)

    def scatter(b):
        at = lane_aligned(b, 256)
        index = jnp.concatenate([conn_ref[a : a + 1, at] for a in range(4)], axis=1) - 256 * b
        hot = onehot(256, index & 255)
        upper = (index >> 8).astype(F32)
        value = jnp.concatenate(
            [
                spread[a, pl.ds(pl.multiple_of(16 * b + 8 * h, 8), 8), :]
                for a in range(4)
                for h in range(2)
            ],
            axis=1,
        )
        high = value * upper
        both = split(value - high, 2) + split(high, 2)
        found = dot(jnp.concatenate(both, axis=0), hot, NT)
        sum_ref[:, at] += found[0:8] + found[8:16]
        sum_ref[:, lane_aligned(b + 1, 256)] += found[16:24] + found[24:32]

    def scatter_step(b, _):
        scatter(2 * b)
        scatter(2 * b + 1)
        return 0

    lax.fori_loop(0, ROWS // 4, scatter_step, 0)


def elements(velocity, low, high, connectivity, shape_grad, area, thickness, limit, stress):
    return pl.pallas_call(
        elements_kernel,
        out_shape=(
            jax.ShapeDtypeStruct((5, 5, NODE_DEV), F32),
            jax.ShapeDtypeStruct((8, NODE_DEV + 256), F32),
        ),
        scratch_shapes=[
            pltpu.VMEM((5 * EXT, 128), F32),
            pltpu.VMEM((4 * ROWS, 128), jnp.int32),
            pltpu.VMEM((8 * ROWS, 128), F32),
            pltpu.VMEM((25 * ROWS, 128), F32),
            pltpu.VMEM((4, 8 * ROWS, 128), F32),
        ],
        compiler_params=pltpu.CompilerParams(vmem_limit_bytes=40 * 2**20),
        name="elements",
    )(velocity, low, high, connectivity, shape_grad, area, thickness, limit, stress)


def contact_kernel(count_ref, node_ref, face_of_ref, faces_ref, nodes_ref, out_ref, table):
    def expand(f, _):
        x = faces_ref[:, lane_aligned(f, 128)]
        r, m, stiff = [x[i : i + 1] for i in range(3)], [x[i : i + 1] for i in range(3, 6)], x[6:7]
        apart = m[0] * r[0] + m[1] * r[1] + m[2] * r[2]
        square = r[0] * r[0] + r[1] * r[1] + r[2] * r[2]
        scaled = [(2.0 / REACH_SQ * LOG2E) * v for v in r]
        strength = stiff * jnp.exp2((-LOG2E / REACH_SQ) * square)
        stacked = jnp.concatenate([*m, apart, *scaled, strength], axis=0).T
        for q in range(8):
            table[f, q] = jnp.broadcast_to(stacked[:, q : q + 1], (128, 128))
        return 0

    lax.fori_loop(0, FACE_TILES, expand, 0)
    out_ref[...] = jnp.zeros_like(out_ref)

    def pair(q, _):
        n, f = node_ref[q], face_of_ref[q]
        x = nodes_ref[n]
        p = [jnp.broadcast_to(x[i : i + 1], (8, 128)) for i in range(3)]
        u = [jnp.broadcast_to(-DAMPING * x[i : i + 1], (8, 128)) for i in range(3, 6)]
        square = x[0:1] * x[0:1] + x[1:2] * x[1:2] + x[2:3] * x[2:3]
        scale = x[6:7] * jnp.exp2((-LOG2E / REACH_SQ) * square)
        total = [jnp.zeros((8, 128), F32) for _ in range(3)]
        for k in range(16):
            mx, my, mz, apart, rx, ry, rz, stiff = [table[f, i, 8 * k : 8 * k + 8] for i in range(8)]
            depth = jnp.maximum(apart - (mx * p[0] + my * p[1] + mz * p[2]), 0.0)
            reach = jnp.exp2(rx * p[0] + ry * p[1] + rz * p[2])
            along = 1.0 + (mx * u[0] + my * u[1] + mz * u[2])
            size = (stiff * reach) * (depth * along)
            total = [t + size * m for t, m in zip(total, (mx, my, mz))]
        force = [scale * jnp.sum(t, axis=0, keepdims=True) for t in total]
        out_ref[n, 0:3] += jnp.concatenate(force, axis=0)
        return 0

    lax.fori_loop(0, count_ref[0], pair, 0)


def contact_forces(count, node, face, faces, nodes):
    smem = pl.BlockSpec(memory_space=pltpu.SMEM)
    vmem = pl.BlockSpec(memory_space=pltpu.VMEM)
    return pl.pallas_call(
        contact_kernel,
        out_shape=jax.ShapeDtypeStruct((DEVICES, 4, 128), F32),
        in_specs=[smem, smem, smem, vmem, vmem],
        scratch_shapes=[pltpu.VMEM((FACE_TILES, 8, 128, 128), F32)],
        compiler_params=pltpu.CompilerParams(vmem_limit_bytes=40 * 2**20),
        name="contact",
    )(count, node, face, faces, nodes)


def finish_kernel(back_ref, owner_ref, rank_ref, sum_ref, low_ref, high_ref, vel_ref, mass_ref, out_ref, side):
    for c in range(3):
        turned = back_ref[pl.ds(c, 128, stride=4), :].T
        for i, part in enumerate(split(turned, 2)):
            side[128 * c : 128 * c + 128, 128 * i : 128 * i + 128] = part

    def block(b):
        at = lane_aligned(b, 256)
        own = onehot(128, owner_ref[0:1, at])
        found = dot(side[...], jnp.concatenate([own, own], axis=0), NN)
        rank = rank_ref[0:1, at].astype(jnp.int32)
        mine = lax.broadcasted_iota(jnp.int32, (128, 256), 0) == rank
        contact = [
            jnp.sum(jnp.where(mine, found[128 * c : 128 * c + 128], 0.0), axis=0, keepdims=True)
            for c in range(3)
        ]
        contact = jnp.concatenate([*contact, jnp.zeros((2, 256), F32)], axis=0)
        inner = sum_ref[0:5, pl.ds(pl.multiple_of(b * 256 + 128, 128), 256)]
        out_ref[:, at] = vel_ref[:, at] + mass_ref[0:1, at] * (contact - inner)

    def step(b, _):
        block(2 * b)
        block(2 * b + 1)
        return 0

    lax.fori_loop(0, NODE_DEV // 512, step, 0)
    for ref, at in ((low_ref, pl.ds(0, 128)), (high_ref, pl.ds(NODE_DEV - 128, 128))):
        out_ref[:, at] -= mass_ref[0:1, at] * ref[0:5, :]


def finish(back, owner, rank, summed, low, high, velocity, inv_mass):
    return pl.pallas_call(
        finish_kernel,
        out_shape=jax.ShapeDtypeStruct((5, NODE_DEV), F32),
        scratch_shapes=[pltpu.VMEM((384, 256), BF)],
        compiler_params=pltpu.CompilerParams(vmem_limit_bytes=40 * 2**20),
        name="finish",
    )(back, owner, rank, summed, low, high, velocity, inv_mass)


AXES = ("dom", "sub")


def neighbours(first, last):
    count = lax.axis_size("dom") * lax.axis_size("sub")
    up = [(i, i + 1) for i in range(count - 1)]
    return lax.ppermute(last, AXES, up), lax.ppermute(first, AXES, [(b, a) for a, b in up])


def body(
    velocity, position, inv_mass, connectivity, shape_grad, area, thickness, yield_stress, stress,
    contact_owner, face_center, face_angle, face_stiffness, ghost_list, pair_node, pair_face,
    pair_count,
):
    owner = contact_owner.reshape(1, NODE_DEV)
    rank, outgoing = slots(owner, position, velocity)
    incoming = lax.all_to_all(outgoing.reshape(DEVICES, 8, 128), AXES, 0, 0, tiled=True)
    azimuth, elevation = face_angle[0], face_angle[1]
    flat = jnp.cos(elevation)
    normal = [jnp.cos(azimuth) * flat, jnp.sin(azimuth) * flat, jnp.sin(elevation)]
    faces = jnp.concatenate(
        [face_center, jnp.stack([*normal, face_stiffness, jnp.zeros_like(face_stiffness)])]
    )
    lent = lend(ghost_list.reshape(1, 2 * GHOST), faces)
    before, after = neighbours(lent[:, :GHOST], lent[:, GHOST:])
    all_faces = jnp.concatenate([before, faces, after], axis=1)
    low, high = neighbours(velocity[:, :HALO], velocity[:, NODE_DEV - HALO :])
    square = (ROWS, 128)
    new_stress, summed = elements(
        velocity, low, high, connectivity, shape_grad, area.reshape(square),
        thickness.reshape(square), yield_stress.reshape(square), stress,
    )
    below, above = neighbours(summed[:, :HALO], summed[:, HALO + NODE_DEV :])
    forces = contact_forces(pair_count, pair_node, pair_face, all_faces, incoming)
    back = lax.all_to_all(forces, AXES, 0, 0, tiled=True)
    new_velocity = finish(
        back.reshape(DEVICES * 4, 128), owner, rank, summed, below, above, velocity,
        inv_mass.reshape(1, NODE_DEV),
    )
    return new_velocity, new_stress


def solution(mesh):
    nodes, rows = P(AXES), P(None, AXES)
    in_specs = (
        rows, rows, nodes, rows, P(None, None, AXES), nodes, nodes, nodes, P(None, None, AXES),
        P(AXES, None), rows, rows, nodes, nodes, nodes, nodes, nodes,
    )
    out_specs = (rows, P(None, None, AXES))
    return jax.shard_map(body, mesh=mesh, in_specs=in_specs, out_specs=out_specs, check_vma=False)
```

time: 323 us -> 110 us (0.34)
  the two profiles are of different devices: /device:TPU:1 before, /device:TPU:32 now
where the time goes in v1:
time: 110 us
  Pallas kernels  48.3 us (44%)
  starting transfers between devices  41.1 us (37%)
  waiting for transfers between devices  13.1 us (12%)
  local copies, waits for them, and re-layouts  4.11 us (4%)
  between operations  1.53 us (1%)
  other arithmetic  1.32 us (1%)
    pallas_call x1, Pallas kernels, contact_forces(): pl.pallas_call(contact_kernel, out_shape=jax.ShapeDtypeStruct((DEVICES, 4...  18.2 us
    ppermute x3, starting transfers between devices, neighbours(): lax.ppermute(first, AXES, [(b, a) for a, b in up])  14.7 us
    ppermute x3, waiting for transfers between devices, neighbours(): lax.ppermute(last, AXES, up)  12.4 us
    pallas_call x1, Pallas kernels, elements(): pl.pallas_call(elements_kernel, out_shape=(jax.ShapeDtypeStruct((5, 5, NO...  11.6 us
    pallas_call x1, Pallas kernels, slots(): pl.pallas_call(slots_kernel, out_shape=(jax.ShapeDtypeStruct((1, NODE_DEV...  11.4 us
    all_to_all x1, starting transfers between devices, body(): lax.all_to_all(outgoing.reshape(DEVICES, 8, 128), AXES, 0, 0, tiled=True)  10.2 us
    ppermute x3, starting transfers between devices, neighbours(): lax.ppermute(last, AXES, up)  9.22 us
    all_to_all x1, starting transfers between devices, body(): back = lax.all_to_all(forces, AXES, 0, 0, tiled=True)  6.97 us
  transfers between devices with their start and end apart: 8, of which 3 were waited for; matrix products, arithmetic and copies ran while one was open for 3% of the time, Pallas kernels for 12%

profile of v1, /device:TPU:32, one launch (start us, length us, event | category | flops | bytes accessed | tf_op | source)
XLA Modules:
  0.0 109.5 jit_solution(6587393597934558260)
XLA Ops:
  0.6 0.0 copy-start.13
  0.6 0.0 copy-start.12
  0.7 0.0 copy-start
  0.7 1.0 copy-done
  1.6 0.0 copy-start.5
  1.6 0.9 copy-done.5
  2.5 0.0 copy-start.6
  2.5 0.8 copy-done.6
  3.3 0.0 copy-start.15
  3.3 0.0 copy-start.14
  3.3 0.0 copy-start.16
  3.3 11.4 %slots.1 = (f32[1,8192]{1,0:T(1,128)S(1)}, f32[1024,128]{1,0:T(8,128)}) custom-call(s32[1,8192]{1,0:T(1,128)S(1)} %bitcast.10, f32[3,8192]{1,0:T(4,128)S(1)} %copy-done.5, f32[5,8192]{1,0:T(8,128)S(1)} %copy-done), custom_call_target="tpu_custom_call" | custom-call | tf_op jit(solution)/shard_map/slots/pallas_call | solution.py:121
  14.7 0.0 copy-start.1
  14.7 0.0 copy-start.2
  14.7 0.0 copy-start.3
  14.7 0.0 copy-start.4
  14.7 0.0 copy-start.8
  14.8 0.0 copy-start.9
  14.8 0.0 copy-start.10
  14.8 10.2 %all-to-all-start = ((f32[128,8,128]{2,1,0:T(8,128)}), f32[128,8,128]{2,1,0:T(8,128)S(1)}, u32[]{:S(2)}, u32[]{:S(2)}) async-start(f32[128,8,128]{2,1,0:T(8,128)} %bitcast.3), calls=%async_computation | async-start | bytes 1048576 | tf_op jit(solution)/shard_map/all_to_all | solution.py:428
  25.0 0.0 copy-done.15
  25.0 0.5 slice_sine_fusion
  25.5 0.0 copy-done.14
  25.5 0.0 copy-done.16
  25.5 0.7 concatenate.6.face_ref
  26.2 1.6 %lend.1 = f32[8,512]{1,0:T(8,128)} custom-call(s32[1,512]{1,0:T(1,128)} %bitcast.17, f32[8,2048]{1,0:T(8,128)} %concatenate.6.face_ref), custom_call_target="tpu_custom_call" | custom-call | tf_op jit(solution)/shard_map/lend/pallas_call | solution.py:149
  27.8 0.7 fusion.2
  28.6 3.4 %collective-permute-start = (f32[8,256]{1,0:T(8,128)S(1)}, f32[8,256]{1,0:T(8,128)S(1)}, u32[]{:S(2)}, u32[]{:S(2)}) collective-permute-start(f32[8,256]{1,0:T(8,128)S(1)} %get-tuple-element.14), channel_id=1, source_target_pairs={{0,1},{1,2},{2,3},{3,4},{4,5},{5,6},{6,7},{7,8},{8,9},{9,10},{10,1... | collective-permute-start | bytes 24584 | tf_op jit(solution)/shard_map/ppermute | solution.py:418
  31.9 6.4 %collective-permute-start.1 = (f32[8,256]{1,0:T(8,128)S(1)}, f32[8,256]{1,0:T(8,128)S(1)}, u32[]{:S(2)}, u32[]{:S(2)}) collective-permute-start(f32[8,256]{1,0:T(8,128)S(1)} %get-tuple-element.15), channel_id=1, source_target_pairs={{1,0},{2,1},{3,2},{4,3},{5,4},{6,5},{7,6},{8,7},{9,8},{10,9},{11,1... | collective-permute-start | bytes 24584 | tf_op jit(solution)/shard_map/ppermute | solution.py:418
  39.0 0.0 collective-permute-done
  39.0 0.7 collective-permute-done.1
  39.7 0.8 pad_maximum_fusion.faces_ref
  40.5 0.0 all-to-all-done.nodes_ref
  40.5 0.0 copy-done.13
  40.6 0.0 copy-done.12
  40.6 18.2 %contact.1 = f32[128,4,128]{2,1,0:T(4,128)} custom-call(s32[1]{0:T(128)S(6)} %copy.19.count_ref, s32[128]{0:T(128)S(1)} %copy-done.12, s32[128]{0:T(128)S(1)} %copy-done.13, f32[8,2560]{1,0:T(8,128)S(1)} %pad_maximum_fusion.faces_ref, f32[128,8,128]{2,1,0:T(8,128)S(1)} %all-to-all-done.nodes_ref), custom_call_target="tpu_custom_call" | custom-call | tf_op jit(solution)/shard_map/contact/pallas_call | solution.py:362
  58.8 0.0 copy-start.7
  58.8 0.0 copy-start.11
  58.8 7.0 %all-to-all-start.1 = ((f32[128,4,128]{2,1,0:T(4,128)}), f32[128,4,128]{2,1,0:T(4,128)S(1)}, u32[]{:S(2)}, u32[]{:S(2)}) async-start(f32[128,4,128]{2,1,0:T(4,128)} %contact.1), calls=%async_computation.1 | async-start | bytes 524288 | tf_op jit(solution)/shard_map/all_to_all | solution.py:446
  65.8 0.0 copy-done.1
  65.8 6.4 %collective-permute-start.3 = (f32[5,128]{1,0:T(8,128)S(1)}, f32[5,128]{1,0:T(8,128)S(1)}, u32[]{:S(2)}, u32[]{:S(2)}) collective-permute-start(f32[5,128]{1,0:T(8,128)S(1)} %get-tuple-element.12), channel_id=1, source_target_pairs={{1,0},{2,1},{3,2},{4,3},{5,4},{6,5},{7,6},{8,7},{9,8},{10,9},{11,1... | collective-permute-start | bytes 7688 | tf_op jit(solution)/shard_map/ppermute | solution.py:418
  72.2 1.9 %collective-permute-start.2 = (f32[5,128]{1,0:T(8,128)S(1)}, f32[5,128]{1,0:T(8,128)S(1)}, u32[]{:S(2)}, u32[]{:S(2)}) collective-permute-start(f32[5,128]{1,0:T(8,128)S(1)} %get-tuple-element.13), channel_id=1, source_target_pairs={{0,1},{1,2},{2,3},{3,4},{4,5},{5,6},{6,7},{7,8},{8,9},{9,10},{10,1... | collective-permute-start | bytes 7688 | tf_op jit(solution)/shard_map/ppermute | solution.py:418
  74.1 0.0 collective-permute-done.3.high_ref
  74.1 7.2 %collective-permute-done.2.low_ref = f32[5,128]{1,0:T(8,128)S(1)} collective-permute-done((f32[5,128]{1,0:T(8,128)S(1)}, f32[5,128]{1,0:T(8,128)S(1)}, u32[]{:S(2)}, u32[]{:S(2)}) %collective-permute-start.2) | collective-permute-done | bytes 2592 | tf_op jit(solution)/shard_map/ppermute | solution.py:418
  81.4 0.0 copy-done.2
  81.4 0.0 copy-done.3
  81.4 0.0 copy-done.4
  81.4 0.0 copy-done.8
  81.4 0.0 copy-done.9
  81.4 0.0 copy-done.10
  81.4 11.6 %elements.1 = (f32[5,5,8192]{2,1,0:T(8,128)}, f32[8,8448]{1,0:T(8,128)S(1)}) custom-call(f32[5,8192]{1,0:T(8,128)S(1)} %copy-done.1, f32[5,128]{1,0:T(8,128)S(1)} %collective-permute-done.2.low_ref, f32[5,128]{1,0:T(8,128)S(1)} %collective-permute-done.3.high_ref, s32[4,8192]{1,0:T(4,128)S(1)} %copy-done.4, f32[2,4,8192]{2,1,0:T(4,128)S(1)} %copy-done.3, ...), custom_call_target="tpu_custom_call" | custom-call | tf_op jit(solution)/shard_map/elements/pallas_call | solution.py:303
  93.0 1.9 %collective-permute-start.5 = (f32[8,128]{1,0:T(8,128)S(1)}, f32[8,128]{1,0:T(8,128)S(1)}, u32[]{:S(2)}, u32[]{:S(2)}) collective-permute-start(f32[8,128]{1,0:T(8,128)S(1)} %get-tuple-element.10), channel_id=1, source_target_pairs={{1,0},{2,1},{3,2},{4,3},{5,4},{6,5},{7,6},{8,7},{9,8},{10,9},{11,1... | collective-permute-start | bytes 12296 | tf_op jit(solution)/shard_map/ppermute | solution.py:418
  94.9 3.9 %collective-permute-start.4 = (f32[8,128]{1,0:T(8,128)S(1)}, f32[8,128]{1,0:T(8,128)S(1)}, u32[]{:S(2)}, u32[]{:S(2)}) collective-permute-start(f32[8,128]{1,0:T(8,128)S(1)} %get-tuple-element.11), channel_id=1, source_target_pairs={{0,1},{1,2},{2,3},{3,4},{4,5},{5,6},{6,7},{7,8},{8,9},{9,10},{10,1... | collective-permute-start | bytes 12296 | tf_op jit(solution)/shard_map/ppermute | solution.py:418
  98.8 0.0 collective-permute-done.5.high_ref
  98.9 5.2 %collective-permute-done.4.low_ref = f32[8,128]{1,0:T(8,128)S(1)} collective-permute-done((f32[8,128]{1,0:T(8,128)S(1)}, f32[8,128]{1,0:T(8,128)S(1)}, u32[]{:S(2)}, u32[]{:S(2)}) %collective-permute-start.4) | collective-permute-done | bytes 4128 | tf_op jit(solution)/shard_map/ppermute | solution.py:418
  104.1 0.0 all-to-all-done.1
  104.1 0.0 copy-done.7
  104.1 0.0 copy-done.11
  104.1 5.4 %finish.1 = f32[5,8192]{1,0:T(8,128)} custom-call(f32[512,128]{1,0:T(8,128)S(1)} %bitcast.9, s32[1,8192]{1,0:T(1,128)S(1)} %bitcast.11, f32[1,8192]{1,0:T(1,128)S(1)} %get-tuple-element.7.rank_ref, f32[8,8448]{1,0:T(8,128)S(1)} %get-tuple-element.8.sum_ref, f32[8,128]{1,0:T(8,128)S(1)} %collective-permute-done.4.low_ref, ...), custom_call_target="tpu_custom_call" | custom-call | tf_op jit(solution)/shard_map/finish/pallas_call | solution.py:403
  (3 shorter events, 0.0 us)
Async XLA Ops:
  0.6 39.9 %copy-start.13 = (s32[128]{0:T(128)S(1)}, s32[128]{0:T(128)}, u32[]{:S(2)}) copy-start(s32[128]{0:T(128)} %face_of_ref.1) | copy-start | bytes 1540
  0.6 39.9 %copy-start.12 = (s32[128]{0:T(128)S(1)}, s32[128]{0:T(128)}, u32[]{:S(2)}) copy-start(s32[128]{0:T(128)} %node_ref.1) | copy-start | bytes 1540
  0.7 1.0 copy-start
  1.6 0.9 copy-start.5
  2.5 0.8 copy-start.6
  3.3 21.7 %copy-start.15 = (f32[2,2048]{1,0:T(2,128)S(1)}, f32[2,2048]{1,0:T(2,128)}, u32[]{:S(2)}) copy-start(f32[2,2048]{1,0:T(2,128)} %param.28) | copy-start | bytes 49156
  3.3 22.2 %copy-start.14 = (f32[3,2048]{1,0:T(4,128)S(1)}, f32[3,2048]{1,0:T(4,128)}, u32[]{:S(2)}) copy-start(f32[3,2048]{1,0:T(4,128)} %param.27) | copy-start | bytes 73732
  3.3 22.2 %copy-start.16 = (f32[2048]{0:T(1024)S(1)}, f32[2048]{0:T(1024)}, u32[]{:S(2)}) copy-start(f32[2048]{0:T(1024)} %param.29) | copy-start | bytes 24580
  14.7 51.0 %copy-start.1 = (f32[5,8192]{1,0:T(8,128)S(1)}, f32[5,8192]{1,0:T(8,128)}, u32[]{:S(2)}) copy-start(f32[5,8192]{1,0:T(8,128)} %vel_ref.5) | copy-start | bytes 491524
  14.7 66.6 %copy-start.2 = (f32[5,5,8192]{2,1,0:T(8,128)S(1)}, f32[5,5,8192]{2,1,0:T(8,128)}, u32[]{:S(2)}) copy-start(f32[5,5,8192]{2,1,0:T(8,128)} %stress_ref.1) | copy-start | bytes 2457604
  14.7 66.6 %copy-start.3 = (f32[2,4,8192]{2,1,0:T(4,128)S(1)}, f32[2,4,8192]{2,1,0:T(4,128)}, u32[]{:S(2)}) copy-start(f32[2,4,8192]{2,1,0:T(4,128)} %grad_ref.1) | copy-start | bytes 786436
  14.7 66.6 %copy-start.4 = (s32[4,8192]{1,0:T(4,128)S(1)}, s32[4,8192]{1,0:T(4,128)}, u32[]{:S(2)}) copy-start(s32[4,8192]{1,0:T(4,128)} %conn_ref.1) | copy-start | bytes 393220
  14.7 66.6 %copy-start.8 = (f32[8192]{0:T(1024)S(1)}, f32[8192]{0:T(1024)}, u32[]{:S(2)}) copy-start(f32[8192]{0:T(1024)} %param.22) | copy-start | bytes 98308
  14.8 66.6 %copy-start.9 = (f32[8192]{0:T(1024)S(1)}, f32[8192]{0:T(1024)}, u32[]{:S(2)}) copy-start(f32[8192]{0:T(1024)} %param.23) | copy-start | bytes 98308
  14.8 66.6 %copy-start.10 = (f32[8192]{0:T(1024)S(1)}, f32[8192]{0:T(1024)}, u32[]{:S(2)}) copy-start(f32[8192]{0:T(1024)} %param.24) | copy-start | bytes 98308
  14.8 25.8 %all-to-all-start = ((f32[128,8,128]{2,1,0:T(8,128)}), f32[128,8,128]{2,1,0:T(8,128)S(1)}, u32[]{:S(2)}, u32[]{:S(2)}) async-start(f32[128,8,128]{2,1,0:T(8,128)} %bitcast.3), calls=%async_computation | async-start | bytes 1048576 | tf_op jit(solution)/shard_map/all_to_all | solution.py:428
  28.6 10.4 %collective-permute-start = (f32[8,256]{1,0:T(8,128)S(1)}, f32[8,256]{1,0:T(8,128)S(1)}, u32[]{:S(2)}, u32[]{:S(2)}) collective-permute-start(f32[8,256]{1,0:T(8,128)S(1)} %get-tuple-element.14), channel_id=1, source_target_pairs={{0,1},{1,2},{2,3},{3,4},{4,5},{5,6},{6,7},{7,8},{8,9},{9,10},{10,1... | collective-permute-start | bytes 24584 | tf_op jit(solution)/shard_map/ppermute | solution.py:418
  31.9 7.7 %collective-permute-start.1 = (f32[8,256]{1,0:T(8,128)S(1)}, f32[8,256]{1,0:T(8,128)S(1)}, u32[]{:S(2)}, u32[]{:S(2)}) collective-permute-start(f32[8,256]{1,0:T(8,128)S(1)} %get-tuple-element.15), channel_id=1, source_target_pairs={{1,0},{2,1},{3,2},{4,3},{5,4},{6,5},{7,6},{8,7},{9,8},{10,9},{11,1... | collective-permute-start | bytes 24584 | tf_op jit(solution)/shard_map/ppermute | solution.py:418
  58.8 45.3 %copy-start.7 = (s32[8192,1]{0,1:T(1,128)S(1)}, s32[8192,1]{0,1:T(1,128)}, u32[]{:S(2)}) copy-start(s32[8192,1]{0,1:T(1,128)} %param.26) | copy-start | bytes 98308
  58.8 45.3 %copy-start.11 = (f32[8192]{0:T(1024)S(1)}, f32[8192]{0:T(1024)}, u32[]{:S(2)}) copy-start(f32[8192]{0:T(1024)} %param.19) | copy-start | bytes 98308
  58.8 45.3 %all-to-all-start.1 = ((f32[128,4,128]{2,1,0:T(4,128)}), f32[128,4,128]{2,1,0:T(4,128)S(1)}, u32[]{:S(2)}, u32[]{:S(2)}) async-start(f32[128,4,128]{2,1,0:T(4,128)} %contact.1), calls=%async_computation.1 | async-start | bytes 524288 | tf_op jit(solution)/shard_map/all_to_all | solution.py:446
  65.8 8.4 %collective-permute-start.3 = (f32[5,128]{1,0:T(8,128)S(1)}, f32[5,128]{1,0:T(8,128)S(1)}, u32[]{:S(2)}, u32[]{:S(2)}) collective-permute-start(f32[5,128]{1,0:T(8,128)S(1)} %get-tuple-element.12), channel_id=1, source_target_pairs={{1,0},{2,1},{3,2},{4,3},{5,4},{6,5},{7,6},{8,7},{9,8},{10,9},{11,1... | collective-permute-start | bytes 7688 | tf_op jit(solution)/shard_map/ppermute | solution.py:418
  72.2 9.1 %collective-permute-start.2 = (f32[5,128]{1,0:T(8,128)S(1)}, f32[5,128]{1,0:T(8,128)S(1)}, u32[]{:S(2)}, u32[]{:S(2)}) collective-permute-start(f32[5,128]{1,0:T(8,128)S(1)} %get-tuple-element.13), channel_id=1, source_target_pairs={{0,1},{1,2},{2,3},{3,4},{4,5},{5,6},{6,7},{7,8},{8,9},{9,10},{10,1... | collective-permute-start | bytes 7688 | tf_op jit(solution)/shard_map/ppermute | solution.py:418
  93.0 5.8 %collective-permute-start.5 = (f32[8,128]{1,0:T(8,128)S(1)}, f32[8,128]{1,0:T(8,128)S(1)}, u32[]{:S(2)}, u32[]{:S(2)}) collective-permute-start(f32[8,128]{1,0:T(8,128)S(1)} %get-tuple-element.10), channel_id=1, source_target_pairs={{1,0},{2,1},{3,2},{4,3},{5,4},{6,5},{7,6},{8,7},{9,8},{10,9},{11,1... | collective-permute-start | bytes 12296 | tf_op jit(solution)/shard_map/ppermute | solution.py:418
  94.9 9.1 %collective-permute-start.4 = (f32[8,128]{1,0:T(8,128)S(1)}, f32[8,128]{1,0:T(8,128)S(1)}, u32[]{:S(2)}, u32[]{:S(2)}) collective-permute-start(f32[8,128]{1,0:T(8,128)S(1)} %get-tuple-element.11), channel_id=1, source_target_pairs={{0,1},{1,2},{2,3},{3,4},{4,5},{5,6},{6,7},{7,8},{8,9},{9,10},{10,1... | collective-permute-start | bytes 12296 | tf_op jit(solution)/shard_map/ppermute | solution.py:418

commit v2 on v1

v2 whole, which is shorter than its diff:
```python
import functools

import jax
import jax.numpy as jnp
from jax import lax
from jax.experimental import pallas as pl
from jax.experimental.pallas import tpu as pltpu
from jax.sharding import PartitionSpec as P

TILE = 128
HALO = 128
GHOST = 256
NODE_DEV = 8192
ROWS = NODE_DEV // 128
FACE_DEV = 2048
FACE_TILES = 20
DEVICES = 128
PAIRS = 128
EXT = ROWS + 8

LOBATTO_POINTS = (-1.0, -0.6546536707079771, 0.0, 0.6546536707079771, 1.0)
LOBATTO_WEIGHTS = (0.1, 49.0 / 90.0, 32.0 / 45.0, 49.0 / 90.0, 0.1)
PLANE_MODULUS = 1.0 / 0.91
POISSON = 0.3
SHEAR_MODULUS = 5.0 / 6.0 / 2.6
DAMPING = 0.3
REACH_SQ = 0.5
LOG2E = 1.4426950408889634

BF = jnp.bfloat16
F32 = jnp.float32
NT = (((1,), (1,)), ((), ()))
NN = (((1,), (0,)), ((), ()))


def dot(a, b, dims):
    return lax.dot_general(a, b, dims, preferred_element_type=F32)


def onehot(count, row):
    where = lax.broadcasted_iota(jnp.int32, (count, row.shape[1]), 0)
    return jnp.where(where == row, 1.0, 0.0).astype(BF)


def split(x, parts):
    out = []
    for _ in range(parts - 1):
        head = x.astype(BF)
        out.append(head)
        x = x - head.astype(F32)
    out.append(x.astype(BF))
    return out


def lane_aligned(x, size):
    return pl.ds(pl.multiple_of(x * size, size), size)


NODE_PARTS = 3
MESH = pl.DeviceIdType.MESH


def constitutive(corner, grad_x, grad_y, area, thickness, limit, old):
    def over(f):
        total = f(0)
        for a in range(1, 4):
            total = total + f(a)
        return total

    vx, vy, vz, rx, ry = corner
    memb_xx = over(lambda a: grad_x[a] * vx[a])
    bend_xx = over(lambda a: grad_x[a] * ry[a])
    memb_yy = over(lambda a: grad_y[a] * vy[a])
    bend_yy = -over(lambda a: grad_y[a] * rx[a])
    memb_xy = over(lambda a: grad_y[a] * vx[a] + grad_x[a] * vy[a])
    bend_xy = over(lambda a: grad_y[a] * ry[a] - grad_x[a] * rx[a])
    shear_xz = over(lambda a: grad_x[a] * vz[a]) + 0.25 * over(lambda a: ry[a])
    shear_yz = over(lambda a: grad_y[a] * vz[a]) - 0.25 * over(lambda a: rx[a])
    add_xz, add_yz = SHEAR_MODULUS * shear_xz, SHEAR_MODULUS * shear_yz
    half = 0.5 * thickness
    volume = half * area
    new, force, moment = [], [0.0] * 5, [0.0] * 3
    for layer in range(5):
        height = half * LOBATTO_POINTS[layer]
        exx = memb_xx + height * bend_xx
        eyy = memb_yy + height * bend_yy
        exy = memb_xy + height * bend_xy
        t0 = old(layer, 0) + PLANE_MODULUS * (exx + POISSON * eyy)
        t1 = old(layer, 1) + PLANE_MODULUS * (eyy + POISSON * exx)
        t2 = old(layer, 2) + PLANE_MODULUS * 0.5 * (1.0 - POISSON) * exy
        t3 = old(layer, 3) + add_xz
        t4 = old(layer, 4) + add_yz
        plus, minus = t0 + t1, t0 - t1
        mises = jnp.sqrt(
            0.25 * (plus * plus) + 0.75 * (minus * minus) + 3.0 * (t2 * t2 + t3 * t3 + t4 * t4)
        )
        factor = limit / jnp.maximum(mises, limit)
        updated = [t * factor for t in (t0, t1, t2, t3, t4)]
        new.append(updated)
        weight = LOBATTO_WEIGHTS[layer] * volume
        weighted = [weight * u for u in updated]
        force = [f + w for f, w in zip(force, weighted)]
        moment = [m + height * w for m, w in zip(moment, weighted)]
    corners = []
    for a in range(4):
        gx, gy = grad_x[a], grad_y[a]
        corners.append(
            [
                gx * force[0] + gy * force[2],
                gy * force[1] + gx * force[2],
                gx * force[3] + gy * force[4],
                -(gy * moment[1] + gx * moment[2]) - 0.25 * force[4],
                gx * moment[0] + gy * moment[2] + 0.25 * force[3],
            ]
        )
    return new, corners


def slots(owner_ref, pos_ref, vel_ref, rank_ref, out_ref, run, acc, tri):
    later = lax.broadcasted_iota(jnp.int32, (256, 384), 0)
    column = lax.broadcasted_iota(jnp.int32, (256, 384), 1)
    tri[...] = jnp.where((later < column) | (column >= 256), 1.0, 0.0).astype(BF)
    run[...] = jnp.zeros_like(run)

    def rank_block(b):
        at = lane_aligned(b, 256)
        own = owner_ref[0:1, at]
        where = lax.broadcasted_iota(jnp.int32, (DEVICES, 256), 0)
        hot = jnp.where(where == own, 1.0, 0.0)
        counts = dot(hot.astype(BF), tri[...], NN)
        base = run[...]
        seen = counts[:, :256] + jnp.concatenate([base, base], axis=1)
        rank_ref[0:1, at] = jnp.sum(hot * seen, axis=0, keepdims=True)
        run[...] = base + counts[:, 256:]

    def rank_step(b, _):
        rank_block(2 * b)
        rank_block(2 * b + 1)
        return 0

    lax.fori_loop(0, NODE_DEV // 512, rank_step, 0)
    acc[...] = jnp.zeros_like(acc)

    def place(b, _):
        at = lane_aligned(b, 1024)
        own = owner_ref[0:1, at]
        column = (own & 1) * 128 + rank_ref[0:1, at].astype(jnp.int32)
        hot = onehot(256, column)
        group = onehot(64, own >> 1)
        rows = []
        for c in range(6):
            value = pos_ref[c : c + 1, at] if c < 3 else vel_ref[c - 3 : c - 2, at]
            rows += [group * part for part in split(value, NODE_PARTS)]
        rows.append(group)
        placed = dot(jnp.concatenate(rows, axis=0), hot, NT)
        for c in range(6):
            first = c * NODE_PARTS * 64
            total = placed[first : first + 64]
            for part in range(1, NODE_PARTS):
                total = total + placed[first + part * 64 : first + part * 64 + 64]
            acc[c * 64 : c * 64 + 64, :] += total
        acc[384:448, :] += placed[6 * NODE_PARTS * 64 :]
        return 0

    lax.fori_loop(0, NODE_DEV // 1024, place, 0)
    for first in range(0, 64, 8):
        for low in range(2):
            for c in range(8):
                rows = pl.ds(first * 16 + low * 8 + c, 8, stride=16)
                if c < 7:
                    part = acc[c * 64 + first : c * 64 + first + 8, low * 128 : low * 128 + 128]
                else:
                    part = jnp.zeros((8, 128), F32)
                out_ref[rows, :] = part


def lend(list_ref, face_ref, out_ref):
    for g in range(4):
        index = jnp.broadcast_to(list_ref[:, 128 * g : 128 * g + 128], (8, 128))
        low, high = index & 127, index >> 7
        found = jnp.zeros((8, 128), F32)
        for t in range(FACE_DEV // 128):
            part = jnp.take_along_axis(face_ref[:, 128 * t : 128 * t + 128], low, axis=1)
            found = jnp.where(high == t, part, found)
        out_ref[:, 128 * g : 128 * g + 128] = found


def unpack(vel_ref, conn_ref, grad_ref, stress_ref, vel, conn, grad, stress):
    def step(j, _):
        at = lane_aligned(j, 128)
        vel[pl.ds(j + 1, 5, stride=EXT), :] = vel_ref[:, at]
        conn[pl.ds(j, 4, stride=ROWS), :] = conn_ref[:, at] - 128 * j
        for axis in range(2):
            grad[pl.ds(axis * 4 * ROWS + j, 4, stride=ROWS), :] = grad_ref[axis, :, at]
        for layer in range(5):
            stress[pl.ds(layer * 5 * ROWS + j, 5, stride=ROWS), :] = stress_ref[layer, :, at]
        return 0

    lax.fori_loop(0, ROWS, step, 0, unroll=8)


def elements(vel, conn, grad, area_ref, thick_ref, limit_ref, stress, spread):
    spread[...] = jnp.zeros_like(spread)

    def group(g, _):
        def rows(field):
            return pl.ds(pl.multiple_of(field * ROWS + 8 * g, 8), 8)

        here = pl.ds(pl.multiple_of(8 * g, 8), 8)
        index = [conn[rows(a), :] for a in range(4)]
        low = [i & 127 for i in index]
        part_of = [i >> 7 for i in index]
        corner = []
        for c in range(5):
            window = [vel[pl.ds(c * EXT + 8 * g + k, 8), :] for k in range(3)]
            values = []
            for a in range(4):
                got = [jnp.take_along_axis(w, low[a], axis=1) for w in window]
                values.append(
                    jnp.where(part_of[a] == 0, got[0], jnp.where(part_of[a] == 1, got[1], got[2]))
                )
            corner.append(values)
        grad_x = [grad[rows(a), :] for a in range(4)]
        grad_y = [grad[rows(4 + a), :] for a in range(4)]
        new, forces = constitutive(
            corner, grad_x, grad_y, area_ref[here, :], thick_ref[here, :], limit_ref[here, :],
            lambda layer, c: stress[rows(5 * layer + c), :],
        )
        for layer in range(5):
            for c in range(5):
                stress[rows(5 * layer + c), :] = new[layer][c]
        for a in range(4):
            for c in range(5):
                spread[a, pl.ds(64 * g + c, 8, stride=8), :] = forces[a][c]
        return 0

    lax.fori_loop(0, 8, group, 0)


def pack(stress, new_ref):
    def step(j, _):
        at = lane_aligned(j, 128)
        for layer in range(5):
            new_ref[layer, :, at] = stress[pl.ds(layer * 5 * ROWS + j, 5, stride=ROWS), :]
        return 0

    lax.fori_loop(0, ROWS, step, 0, unroll=8)


def scatter(b, conn_ref, spread, sum_ref):
    at = lane_aligned(b, 256)
    index = jnp.concatenate([conn_ref[a : a + 1, at] for a in range(4)], axis=1) - 256 * b
    hot = onehot(256, index & 255)
    upper = (index >> 8).astype(F32)
    value = jnp.concatenate(
        [spread[a, lane_aligned(2 * b + h, 8), :] for a in range(4) for h in range(2)], axis=1
    )
    high = value * upper
    both = split(value - high, 2) + split(high, 2)
    found = dot(jnp.concatenate(both, axis=0), hot, NT)
    sum_ref[:, at] += found[0:8] + found[8:16]
    sum_ref[:, lane_aligned(b + 1, 256)] += found[16:24] + found[24:32]


def expand(f, faces_ref, table):
    x = faces_ref[:, lane_aligned(f, 128)]
    r, m, stiff = [x[i : i + 1] for i in range(3)], [x[i : i + 1] for i in range(3, 6)], x[6:7]
    apart = m[0] * r[0] + m[1] * r[1] + m[2] * r[2]
    square = r[0] * r[0] + r[1] * r[1] + r[2] * r[2]
    scaled = [(2.0 / REACH_SQ * LOG2E) * v for v in r]
    strength = stiff * jnp.exp2((-LOG2E / REACH_SQ) * square)
    stacked = jnp.concatenate([*m, apart, *scaled, strength], axis=0).T
    for q in range(8):
        table[f, q] = jnp.broadcast_to(stacked[:, q : q + 1], (128, 128))


def pair_force(x, faces_of):
    p = [jnp.broadcast_to(x[i : i + 1], (8, 128)) for i in range(3)]
    u = [jnp.broadcast_to(-DAMPING * x[i : i + 1], (8, 128)) for i in range(3, 6)]
    square = x[0:1] * x[0:1] + x[1:2] * x[1:2] + x[2:3] * x[2:3]
    scale = x[6:7] * jnp.exp2((-LOG2E / REACH_SQ) * square)
    total = [jnp.zeros((8, 128), F32) for _ in range(3)]
    for k in range(16):
        mx, my, mz, apart, rx, ry, rz, stiff = [faces_of(i, k) for i in range(8)]
        depth = jnp.maximum(apart - (mx * p[0] + my * p[1] + mz * p[2]), 0.0)
        reach = jnp.exp2(rx * p[0] + ry * p[1] + rz * p[2])
        along = 1.0 + (mx * u[0] + my * u[1] + mz * u[2])
        size = (stiff * reach) * (depth * along)
        total = [t + size * m for t, m in zip(total, (mx, my, mz))]
    return [scale * jnp.sum(t, axis=0, keepdims=True) for t in total]


def finish(back_ref, owner_ref, rank_ref, sum_ref, vel_ref, mass_ref, out_ref, side):
    for c in range(3):
        turned = back_ref[pl.ds(c, 128, stride=8), :].T
        for i, part in enumerate(split(turned, 2)):
            side[128 * c : 128 * c + 128, 128 * i : 128 * i + 128] = part

    def block(b):
        at = lane_aligned(b, 256)
        own = onehot(128, owner_ref[0:1, at])
        found = dot(side[...], jnp.concatenate([own, own], axis=0), NN)
        rank = rank_ref[0:1, at].astype(jnp.int32)
        mine = lax.broadcasted_iota(jnp.int32, (128, 256), 0) == rank
        contact = [
            jnp.sum(jnp.where(mine, found[128 * c : 128 * c + 128], 0.0), axis=0, keepdims=True)
            for c in range(3)
        ]
        contact = jnp.concatenate([*contact, jnp.zeros((2, 256), F32)], axis=0)
        inner = sum_ref[0:5, pl.ds(pl.multiple_of(b * 256 + 128, 128), 256)]
        out_ref[:, at] = vel_ref[:, at] + mass_ref[0:1, at] * (contact - inner)

    def step(b, _):
        block(2 * b)
        block(2 * b + 1)
        return 0

    lax.fori_loop(0, NODE_DEV // 512, step, 0)


def step_kernel(
    count_ref, node_ref, face_of_ref, node_row_ref, owner_ref, pos_ref, vel_ref, list_ref, face_ref,
    mass_ref, area_ref, thick_ref, limit_ref, conn_hbm, grad_hbm, stress_hbm,
    out_ref, new_ref,
    conn_in, grad_in, stress_in, rank_ref, run, acc, tri, going, coming, faces, lent, ghost_in,
    vel_in, vel, conn, grad, stress, spread, sum_ref, rim_in, table, pairs, leaving, back, side,
    load_sem, send_sem, recv_sem, edge_send, edge_recv,
):
    sub_count = lax.axis_size("sub")
    me = lax.axis_index("dom") * sub_count + lax.axis_index("sub")

    def device(k):
        to = lax.rem(me + k, DEVICES)
        return to, (lax.div(to, sub_count), lax.rem(to, sub_count))

    loads = [
        pltpu.make_async_copy(src, dst, load_sem.at[i])
        for i, (src, dst) in enumerate(
            ((conn_hbm, conn_in), (grad_hbm, grad_in), (stress_hbm, stress_in))
        )
    ]
    for copy in loads:
        copy.start()
    barrier = pltpu.get_barrier_semaphore()

    def greet(k, _):
        pl.semaphore_signal(barrier, inc=1, device_id=device(k)[1], device_id_type=MESH)
        return 0

    lax.fori_loop(1, DEVICES, greet, 0)
    slots(owner_ref, pos_ref, vel_ref, rank_ref, going, run, acc, tri)
    lend(list_ref, face_ref, lent)
    pl.semaphore_wait(barrier, DEVICES - 1)

    def edges(i, first, last, land):
        pair = []
        for end, (src, k) in enumerate(((last, 1), (first, DEVICES - 1))):
            copy = pltpu.make_async_remote_copy(
                src, land.at[end], edge_send.at[i, end], edge_recv.at[i, end],
                device_id=device(k)[1], device_id_type=MESH,
            )
            copy.start()
            pair.append(copy)
        return pair

    def tile(i):
        return pl.ds(pl.multiple_of(8 * i, 8), 8)

    def exchange(i, src, dst):
        def send(k, _):
            to, where = device(k)
            pltpu.make_async_remote_copy(
                src.at[tile(to)], dst.at[tile(me)], send_sem.at[i], recv_sem.at[i],
                device_id=where, device_id_type=MESH,
            ).start()
            return 0

        lax.fori_loop(1, DEVICES, send, 0)
        dst[tile(me), :] = src[tile(me), :]
        others = pl.ds(0, (DEVICES - 1) * 8)
        return pltpu.make_async_remote_copy(
            src.at[others], dst.at[others], send_sem.at[i], recv_sem.at[i],
            device_id=device(1)[1], device_id_type=MESH,
        )

    halo = edges(0, vel_ref.at[:, 0:HALO], vel_ref.at[:, NODE_DEV - HALO : NODE_DEV], vel_in)
    ghosts = edges(1, lent.at[:, 0:GHOST], lent.at[:, GHOST : 2 * GHOST], ghost_in)
    nodes_move = exchange(0, going, coming)
    for copy in loads:
        copy.wait()
    unpack(vel_ref, conn_in, grad_in, stress_in, vel, conn, grad, stress)
    for copy in halo:
        copy.wait()
    vel[pl.ds(0, 5, stride=EXT), :] = vel_in[0]
    vel[pl.ds(ROWS + 1, 5, stride=EXT), :] = vel_in[1]
    elements(vel, conn, grad, area_ref, thick_ref, limit_ref, stress, spread)
    pack(stress, new_ref)
    for copy in ghosts:
        copy.wait()
    faces[:, 0:GHOST] = jnp.where(me > 0, ghost_in[0], 0.0)
    faces[:, GHOST : GHOST + FACE_DEV] = face_ref[...]
    faces[:, GHOST + FACE_DEV :] = jnp.where(me < DEVICES - 1, ghost_in[1], 0.0)

    def expand_step(f, _):
        expand(f, faces, table)
        return 0

    lax.fori_loop(0, FACE_TILES, expand_step, 0)
    nodes_move.wait()

    tiles = coming.reshape(DEVICES, 8, 128)

    def pair_step(q, _):
        x, f = tiles[node_ref[q]], face_of_ref[q]
        force = pair_force(x, lambda i, k: table[f, i, 8 * k : 8 * k + 8])
        for c in range(3):
            pairs[pl.ds(c * PAIRS + q, 1), :] = force[c]
        return 0

    lax.fori_loop(0, PAIRS, pair_step, 0)
    slot = lax.broadcasted_iota(jnp.int32, (1, PAIRS), 1)
    listed = onehot(DEVICES, jnp.where(slot < count_ref[...], node_row_ref[...], -1))
    listed = jnp.concatenate([listed] * 3, axis=1)
    leaving[...] = jnp.zeros_like(leaving)
    for c in range(3):
        parts = jnp.concatenate(split(pairs[c * PAIRS : (c + 1) * PAIRS, :], 3), axis=0)
        leaving[pl.ds(c, DEVICES, stride=8), :] = dot(listed, parts, NN)
    forces_move = exchange(1, leaving, back)

    sum_ref[...] = jnp.zeros_like(sum_ref)
    scatter(0, conn_in, spread, sum_ref)
    scatter(ROWS // 2 - 1, conn_in, spread, sum_ref)
    rims = edges(
        2, sum_ref.at[:, 0:HALO], sum_ref.at[:, HALO + NODE_DEV : 2 * HALO + NODE_DEV], rim_in
    )

    def scatter_step(b, _):
        scatter(2 * b + 1, conn_in, spread, sum_ref)
        scatter(2 * b + 2, conn_in, spread, sum_ref)
        return 0

    lax.fori_loop(0, ROWS // 4 - 1, scatter_step, 0)
    for copy in rims:
        copy.wait()
    sum_ref[:, HALO : 2 * HALO] += rim_in[0]
    sum_ref[:, NODE_DEV : NODE_DEV + HALO] += rim_in[1]
    forces_move.wait()
    finish(back, owner_ref, rank_ref, sum_ref, vel_ref, mass_ref, out_ref, side)


def body(
    velocity, position, inv_mass, connectivity, shape_grad, area, thickness, yield_stress, stress,
    contact_owner, face_center, face_angle, face_stiffness, ghost_list, pair_node, pair_face,
    pair_count,
):
    azimuth, elevation = face_angle[0], face_angle[1]
    flat = jnp.cos(elevation)
    normal = [jnp.cos(azimuth) * flat, jnp.sin(azimuth) * flat, jnp.sin(elevation)]
    faces = jnp.concatenate(
        [face_center, jnp.stack([*normal, face_stiffness, jnp.zeros_like(face_stiffness)])]
    )
    square = (ROWS, 128)
    smem = pl.BlockSpec(memory_space=pltpu.SMEM)
    vmem = pl.BlockSpec(memory_space=pltpu.VMEM)
    hbm = pl.BlockSpec(memory_space=pl.ANY)
    dma = pltpu.SemaphoreType.DMA
    scratch = [
        ((4, NODE_DEV), jnp.int32), ((2, 4, NODE_DEV), F32), ((5, 5, NODE_DEV), F32),
        ((1, NODE_DEV), F32), ((DEVICES, 128), F32), ((448, 256), F32), ((256, 384), BF),
        ((DEVICES * 8, 128), F32), ((DEVICES * 8, 128), F32), ((8, FACE_TILES * 128), F32),
        ((8, 2 * GHOST), F32), ((2, 8, GHOST), F32), ((2, 5, HALO), F32), ((5 * EXT, 128), F32),
        ((4 * ROWS, 128), jnp.int32), ((8 * ROWS, 128), F32), ((25 * ROWS, 128), F32),
        ((4, 8 * ROWS, 128), F32), ((8, NODE_DEV + 256), F32), ((2, 8, HALO), F32),
        ((FACE_TILES, 8, 128, 128), F32), ((3 * PAIRS, 128), F32), ((DEVICES * 8, 128), F32),
        ((DEVICES * 8, 128), F32), ((384, 256), BF),
    ]
    return pl.pallas_call(
        step_kernel,
        out_shape=(
            jax.ShapeDtypeStruct((5, NODE_DEV), F32),
            jax.ShapeDtypeStruct((5, 5, NODE_DEV), F32),
        ),
        in_specs=[vmem] + [smem] * 2 + [vmem] * 10 + [hbm] * 3,
        out_specs=(vmem, vmem),
        scratch_shapes=[
            *(pltpu.VMEM(shape, kind) for shape, kind in scratch),
            dma((3,)), dma((2,)), dma((2,)), dma((3, 2)), dma((3, 2)),
        ],
        compiler_params=pltpu.CompilerParams(
            vmem_limit_bytes=56 * 2**20, collective_id=0, has_side_effects=True
        ),
        name="crash_step",
    )(
        pair_count.reshape(1, 1), pair_node, pair_face, pair_node.reshape(1, PAIRS),
        contact_owner.reshape(1, NODE_DEV), position, velocity, ghost_list.reshape(1, 2 * GHOST),
        faces, inv_mass.reshape(1, NODE_DEV), area.reshape(square), thickness.reshape(square),
        yield_stress.reshape(square), connectivity, shape_grad, stress,
    )


def solution(mesh):
    axes = ("dom", "sub")
    nodes, rows, cells = P(axes), P(None, axes), P(None, None, axes)
    in_specs = (
        rows, rows, nodes, rows, cells, nodes, nodes, nodes, cells, P(axes, None), rows, rows,
        nodes, nodes, nodes, nodes, nodes,
    )
    return jax.shard_map(
        body, mesh=mesh, in_specs=in_specs, out_specs=(rows, cells), check_vma=False
    )
```

time: 110 us -> 66.5 us (0.60)
  the two profiles are of different devices: /device:TPU:32 before, /device:TPU:0 now
where the time goes in v2:
time: 66.5 us; the launch traced here: 66.2 us
  Pallas kernels  58 us (87%)
  local copies, waits for them, and re-layouts  5.59 us (8%)
  between operations  1.3 us (2%)
  other arithmetic  1.26 us (2%)
    pallas_call x1, Pallas kernels, body(): pl.pallas_call(step_kernel, out_shape=(jax.ShapeDtypeStruct((5, NODE_DEV)...  58 us
    unnamed x2, local copies, waits for them, and re-layouts  4.13 us
    concatenate x1, local copies, waits for them, and re-layouts, body(): jnp.concatenate([face_center, jnp.stack([*normal, face_stiffness, jnp.zer...  1.46 us

profile of v2, /device:TPU:0, one launch (start us, length us, event | category | flops | bytes accessed | tf_op | source)
XLA Modules:
  0.0 66.2 jit_solution(152016286694500462)
XLA Ops:
  1.3 1.3 %slice_sine_fusion = (f32[1,2048]{1,0:T(1,128)S(1)}, f32[1,2048]{1,0:T(1,128)S(1)}, f32[1,2048]{1,0:T(1,128)S(1)}) fusion(f32[2,2048]{1,0:T(2,128)} %param.28), kind=kLoop, calls=%fused_computation.2 | loop fusion | flops 4096 | bytes 40960 | tf_op jit(solution)/shard_map/sin | solution.py:458
  2.6 1.5 %concatenate.3.face_ref = f32[8,2048]{1,0:T(8,128)} concatenate(f32[3,2048]{1,0:T(4,128)} %param.27, f32[1,2048]{1,0:T(1,128)S(1)} %get-tuple-element.4, f32[1,2048]{1,0:T(1,128)S(1)} %get-tuple-element.3, f32[1,2048]{1,0:T(1,128)S(1)} %get-tuple-element.2, f32[1,2048]{1,0:T(1,128)} %bitcast.15, f32[1,2048]{1,0:T(1,128)S(1)} %stack_broadcast_in_dim.3), dimensions={0} | concatenate | bytes 131072 | tf_op jit(solution)/shard_map/concatenate | solution.py:459
  4.0 58.0 %crash_step.1 = (f32[5,8192]{1,0:T(8,128)}, f32[5,5,8192]{2,1,0:T(8,128)}) custom-call(s32[1,1]{1,0:T(1,128)} %bitcast.9.count_ref, s32[128]{0:T(128)} %node_ref.1, s32[128]{0:T(128)} %face_of_ref.1, s32[1,128]{1,0:T(1,128)} %bitcast.17, s32[1,8192]{1,0:T(1,128)} %bitcast.10, f32[3,8192]{1,0:T(4,128)} %pos_ref.1, f32[5,8192]{1,0:T(8,128)} %vel_ref.1, ...), custom_call_target="tpu_custom_call" | custom-call | tf_op jit(solution)/shard_map/crash_step/pallas_call | solution.py:477
  62.0 1.7 %copy.22 = f32[5,8192]{1,0:T(8,128)} copy(f32[5,8192]{1,0:T(8,128)} %get-tuple-element.7) | data formatting | bytes 327680
  63.7 2.5 %copy.23 = f32[5,5,8192]{2,1,0:T(8,128)} copy(f32[5,5,8192]{2,1,0:T(8,128)} %get-tuple-element.8) | data formatting | bytes 1638400
  (1 shorter events, 0.0 us)

commit v3 on v2

v3 whole, which is shorter than its diff:
```python
import functools

import jax
import jax.numpy as jnp
from jax import lax
from jax.experimental import pallas as pl
from jax.experimental.pallas import tpu as pltpu
from jax.sharding import PartitionSpec as P

TILE = 128
HALO = 128
GHOST = 256
NODE_DEV = 8192
ROWS = NODE_DEV // 128
FACE_DEV = 2048
FACE_TILES = 20
DEVICES = 128
PAIRS = 128
EXT = ROWS + 8

LOBATTO_POINTS = (-1.0, -0.6546536707079771, 0.0, 0.6546536707079771, 1.0)
LOBATTO_WEIGHTS = (0.1, 49.0 / 90.0, 32.0 / 45.0, 49.0 / 90.0, 0.1)
PLANE_MODULUS = 1.0 / 0.91
POISSON = 0.3
SHEAR_MODULUS = 5.0 / 6.0 / 2.6
DAMPING = 0.3
REACH_SQ = 0.5
LOG2E = 1.4426950408889634

BF = jnp.bfloat16
F32 = jnp.float32
NT = (((1,), (1,)), ((), ()))
NN = (((1,), (0,)), ((), ()))


def dot(a, b, dims):
    return lax.dot_general(a, b, dims, preferred_element_type=F32)


def onehot(count, row):
    where = lax.broadcasted_iota(jnp.int32, (count, row.shape[1]), 0)
    return jnp.where(where == row, 1.0, 0.0).astype(BF)


def split(x, parts):
    out = []
    for _ in range(parts - 1):
        head = x.astype(BF)
        out.append(head)
        x = x - head.astype(F32)
    out.append(x.astype(BF))
    return out


def lane_aligned(x, size):
    return pl.ds(pl.multiple_of(x * size, size), size)


MESH = pl.DeviceIdType.MESH
RANK_STEP, PLACE_STEP, SPREAD_STEP, FACE_STEP, PAIR_STEP, FINISH_STEP = 8, 4, 8, 10, 8, 8
PARTS = (3, 3, 3, 2, 2, 2, 1)


def constitutive(corner, grad_x, grad_y, area, thickness, limit, old):
    def over(f):
        total = f(0)
        for a in range(1, 4):
            total = total + f(a)
        return total

    vx, vy, vz, rx, ry = corner
    memb_xx = over(lambda a: grad_x[a] * vx[a])
    bend_xx = over(lambda a: grad_x[a] * ry[a])
    memb_yy = over(lambda a: grad_y[a] * vy[a])
    bend_yy = -over(lambda a: grad_y[a] * rx[a])
    memb_xy = over(lambda a: grad_y[a] * vx[a] + grad_x[a] * vy[a])
    bend_xy = over(lambda a: grad_y[a] * ry[a] - grad_x[a] * rx[a])
    shear_xz = over(lambda a: grad_x[a] * vz[a]) + 0.25 * over(lambda a: ry[a])
    shear_yz = over(lambda a: grad_y[a] * vz[a]) - 0.25 * over(lambda a: rx[a])
    add_xz, add_yz = SHEAR_MODULUS * shear_xz, SHEAR_MODULUS * shear_yz
    half = 0.5 * thickness
    volume = half * area
    new, force, moment = [], [0.0] * 5, [0.0] * 3
    for layer in range(5):
        height = half * LOBATTO_POINTS[layer]
        exx = memb_xx + height * bend_xx
        eyy = memb_yy + height * bend_yy
        exy = memb_xy + height * bend_xy
        t0 = old(layer, 0) + PLANE_MODULUS * (exx + POISSON * eyy)
        t1 = old(layer, 1) + PLANE_MODULUS * (eyy + POISSON * exx)
        t2 = old(layer, 2) + PLANE_MODULUS * 0.5 * (1.0 - POISSON) * exy
        t3 = old(layer, 3) + add_xz
        t4 = old(layer, 4) + add_yz
        plus, minus = t0 + t1, t0 - t1
        mises = jnp.sqrt(
            0.25 * (plus * plus) + 0.75 * (minus * minus) + 3.0 * (t2 * t2 + t3 * t3 + t4 * t4)
        )
        factor = limit / jnp.maximum(mises, limit)
        updated = [t * factor for t in (t0, t1, t2, t3, t4)]
        new.append(updated)
        weight = LOBATTO_WEIGHTS[layer] * volume
        weighted = [weight * u for u in updated]
        force = [f + w for f, w in zip(force, weighted)]
        moment = [m + height * w for m, w in zip(moment, weighted)]
    corners = []
    for a in range(4):
        gx, gy = grad_x[a], grad_y[a]
        corners.append(
            [
                gx * force[0] + gy * force[2],
                gy * force[1] + gx * force[2],
                gx * force[3] + gy * force[4],
                -(gy * moment[1] + gx * moment[2]) - 0.25 * force[4],
                gx * moment[0] + gy * moment[2] + 0.25 * force[3],
            ]
        )
    return new, corners


def ranks(owner_ref, rank_ref, run, tri):
    row = lax.broadcasted_iota(jnp.int32, (256, 384), 0)
    column = lax.broadcasted_iota(jnp.int32, (256, 384), 1)
    tri[...] = jnp.where((row < column) | (column >= 256), 1.0, 0.0).astype(BF)
    run[...] = jnp.zeros_like(run)

    def step(b, _):
        spans = [lane_aligned(b * RANK_STEP + i, 256) for i in range(RANK_STEP)]
        where = lax.broadcasted_iota(jnp.int32, (DEVICES, 256), 0)
        hot = [jnp.where(where == owner_ref[0:1, at], 1.0, 0.0) for at in spans]
        counts = dot(jnp.concatenate([h.astype(BF) for h in hot], axis=0), tri[...], NN)
        base = run[...]
        for i, at in enumerate(spans):
            count = counts[DEVICES * i : DEVICES * i + DEVICES]
            seen = count[:, :256] + jnp.concatenate([base, base], axis=1)
            rank_ref[0:1, at] = jnp.sum(hot[i] * seen, axis=0, keepdims=True)
            base = base + count[:, 256:]
        run[...] = base
        return 0

    lax.fori_loop(0, NODE_DEV // (256 * RANK_STEP), step, 0)


def place(owner_ref, rank_ref, pos_ref, vel_ref, out_ref, acc):
    acc[...] = jnp.zeros_like(acc)

    def block(b):
        at = lane_aligned(b, 1024)
        own = owner_ref[0:1, at]
        hot = onehot(256, (own & 1) * 128 + rank_ref[0:1, at].astype(jnp.int32))
        group = onehot(64, own >> 1)
        rows = []
        for c in range(6):
            value = pos_ref[c : c + 1, at] if c < 3 else vel_ref[c - 3 : c - 2, at]
            rows += [group * part for part in split(value, PARTS[c])]
        return dot(jnp.concatenate([*rows, group], axis=0), hot, NT)

    def step(b, _):
        placed = [block(b * PLACE_STEP + i) for i in range(PLACE_STEP)]
        first = 0
        for c, parts in enumerate(PARTS):
            total = acc[c * 64 : c * 64 + 64, :]
            for _ in range(parts):
                for p in placed:
                    total = total + p[first : first + 64]
                first += 64
            acc[c * 64 : c * 64 + 64, :] = total
        return 0

    lax.fori_loop(0, NODE_DEV // (1024 * PLACE_STEP), step, 0)
    for first in range(0, 64, 8):
        for low in range(2):
            for c in range(8):
                if c < 7:
                    part = acc[c * 64 + first : c * 64 + first + 8, low * 128 : low * 128 + 128]
                else:
                    part = jnp.ones((8, 128), F32)
                out_ref[pl.ds(first * 16 + low * 8 + c, 8, stride=16), :] = part


def face_rows(center_ref, angle_ref, stiff_ref, angles, normals, out_ref):
    tiles = FACE_DEV // 128
    for j in range(tiles):
        angles[pl.ds(j, 2, stride=tiles), :] = angle_ref[:, 128 * j : 128 * j + 128]
    azimuth, elevation = angles[0:tiles, :], angles[tiles : 2 * tiles, :]
    flat = jnp.cos(elevation)
    for c, value in enumerate(
        (jnp.cos(azimuth) * flat, jnp.sin(azimuth) * flat, jnp.sin(elevation))
    ):
        normals[pl.ds(c, tiles, stride=8), :] = value
    for j in range(tiles):
        at = slice(128 * j, 128 * j + 128)
        out_ref[:, GHOST + 128 * j : GHOST + 128 * j + 128] = jnp.concatenate(
            [center_ref[:, at], normals[8 * j : 8 * j + 3, :], stiff_ref[:, at], jnp.zeros((1, 128), F32)],
            axis=0,
        )


def lend(list_ref, faces_ref, out_ref):
    for g in range(2 * GHOST // 128):
        index = jnp.broadcast_to(list_ref[:, 128 * g : 128 * g + 128], (8, 128))
        low, high = index & 127, index >> 7
        found = jnp.zeros((8, 128), F32)
        for t in range(FACE_DEV // 128):
            at = slice(GHOST + 128 * t, GHOST + 128 * t + 128)
            part = jnp.take_along_axis(faces_ref[:, at], low, axis=1)
            found = jnp.where(high == t, part, found)
        out_ref[:, 128 * g : 128 * g + 128] = found


def unpack(vel_ref, conn_ref, grad_ref, stress_ref, vel, conn, grad, stress):
    def step(j, _):
        at = lane_aligned(j, 128)
        vel[pl.ds(j + 1, 5, stride=EXT), :] = vel_ref[:, at]
        conn[pl.ds(j, 4, stride=ROWS), :] = conn_ref[:, at] - 128 * j
        for axis in range(2):
            grad[pl.ds(axis * 4 * ROWS + j, 4, stride=ROWS), :] = grad_ref[axis, :, at]
        for layer in range(5):
            stress[pl.ds(layer * 5 * ROWS + j, 5, stride=ROWS), :] = stress_ref[layer, :, at]
        return 0

    lax.fori_loop(0, ROWS, step, 0, unroll=8)


def elements(vel, conn, grad, area_ref, thick_ref, limit_ref, stress, spread):
    spread[...] = jnp.zeros_like(spread)

    def group(g, _):
        def rows(field):
            return pl.ds(pl.multiple_of(field * ROWS + 8 * g, 8), 8)

        here = pl.ds(pl.multiple_of(8 * g, 8), 8)
        index = [conn[rows(a), :] for a in range(4)]
        low = [i & 127 for i in index]
        part_of = [i >> 7 for i in index]
        corner = []
        for c in range(5):
            window = [vel[pl.ds(c * EXT + 8 * g + k, 8), :] for k in range(3)]
            values = []
            for a in range(4):
                got = [jnp.take_along_axis(w, low[a], axis=1) for w in window]
                values.append(
                    jnp.where(part_of[a] == 0, got[0], jnp.where(part_of[a] == 1, got[1], got[2]))
                )
            corner.append(values)
        grad_x = [grad[rows(a), :] for a in range(4)]
        grad_y = [grad[rows(4 + a), :] for a in range(4)]
        new, forces = constitutive(
            corner, grad_x, grad_y, area_ref[here, :], thick_ref[here, :], limit_ref[here, :],
            lambda layer, c: stress[rows(5 * layer + c), :],
        )
        for layer in range(5):
            for c in range(5):
                stress[rows(5 * layer + c), :] = new[layer][c]
        for a in range(4):
            for c in range(5):
                spread[a, pl.ds(64 * g + c, 8, stride=8), :] = forces[a][c]
        return 0

    lax.fori_loop(0, 8, group, 0)


def scatter(b, conn_ref, spread):
    at = lane_aligned(b, 256)
    index = jnp.concatenate([conn_ref[a : a + 1, at] for a in range(4)], axis=1) - 256 * b
    hot = onehot(128, index & 127)
    window = index >> 7
    value = jnp.concatenate(
        [spread[a, lane_aligned(2 * b + h, 8), :] for a in range(4) for h in range(2)], axis=1
    )
    parts = split(value, 2)
    rows = []
    for h in range(4):
        mine = jnp.where(window == h, 1.0, 0.0).astype(BF)
        rows += [part * mine for part in parts]
    found = dot(hot, jnp.concatenate(rows, axis=0), NT).T
    return [found[16 * h : 16 * h + 8] + found[16 * h + 8 : 16 * h + 16] for h in range(4)]


def scatter_blocks(blocks, conn_ref, spread, sum_ref):
    found = [scatter(b, conn_ref, spread) for b in blocks]
    for b, windows in zip(blocks, found):
        for h, window in enumerate(windows):
            sum_ref[:, lane_aligned(2 * b + h, 128)] += window


def six_terms(x):
    high, mid, low = (part.astype(F32) for part in split(x, 3))
    return jnp.concatenate([high, mid, high, mid, low, high], axis=0)


def face_tables(faces_ref, forms, pick, normals):
    row = lax.broadcasted_iota(jnp.int32, (24, 3 * TILE), 0)
    column = lax.broadcasted_iota(jnp.int32, (24, 3 * TILE), 1)
    pick[...] = jnp.where((row & 7) == (column >> 7), 1.0, 0.0).astype(BF)

    def tile(f):
        x = faces_ref[:, lane_aligned(f, TILE)]
        r, m = [x[i : i + 1] for i in range(3)], [x[i : i + 1] for i in range(3, 6)]
        apart = m[0] * r[0] + m[1] * r[1] + m[2] * r[2]
        square = r[0] * r[0] + r[1] * r[1] + r[2] * r[2]
        strength = x[6:7] * jnp.exp2((-LOG2E / REACH_SQ) * square)
        none = jnp.zeros_like(apart)
        depth = [*(-strength * v for v in m), none, none, none, none, strength * apart]
        along = [none, none, none, *(-DAMPING * v for v in m), none, jnp.ones_like(apart)]
        reach = [*((2.0 / REACH_SQ * LOG2E) * v for v in r), none, none, none, none, none]
        for i, form in enumerate((depth, along, reach)):
            terms = six_terms(jnp.concatenate(form, axis=0))
            forms[f, TILE * i : TILE * i + TILE, :] = terms.T.astype(BF)
        parts = [part.astype(F32) for part in split(jnp.concatenate([*m] + [none] * 5, axis=0), 3)]
        wide = dot(jnp.concatenate(parts, axis=0).T.astype(BF), pick[...], NN)
        for i in range(3):
            normals[f, i] = wide[:, TILE * i : TILE * i + TILE]

    def step(b, _):
        for i in range(FACE_STEP):
            tile(b * FACE_STEP + i)
        return 0

    lax.fori_loop(0, FACE_TILES // FACE_STEP, step, 0)


def pair_force(x, form, normal_of):
    high, mid, low = split(x, 3)
    products = dot(form, jnp.concatenate([high, high, mid, mid, high, low], axis=0), NN)
    square = x[0:1] * x[0:1] + x[1:2] * x[1:2] + x[2:3] * x[2:3]
    scale = x[6:7] * jnp.exp2((-LOG2E / REACH_SQ) * square)
    total = [jnp.zeros((8, TILE), F32) for _ in range(3)]
    for k in range(0, TILE, 8):
        depth = jnp.maximum(products[k : k + 8], 0.0)
        along = products[TILE + k : TILE + k + 8]
        size = depth * along * jnp.exp2(products[2 * TILE + k : 2 * TILE + k + 8])
        total = [t + size * normal_of(i, k) for i, t in enumerate(total)]
    return [scale * jnp.sum(t, axis=0, keepdims=True) for t in total]


def step_kernel(*refs):
    inputs, outputs, held, scratch = refs[:17], refs[17:19], refs[19:36], refs[36:]
    (
        owner_ref, pos_ref, vel_ref, center_ref, angle_ref, stiff_ref, list_ref, conn_in, grad_in,
        stress_in, area_ref, thick_ref, limit_ref, node_ref, face_of_ref, node_row_ref, count_ref,
    ) = held
    total_hbm, cells_hbm = outputs
    (
        back, sum_ref, rank_ref, stress, total, side, run, acc, tri, going, coming, angles, unit, faces, lent, ghost_in,
    vel_in, vel, conn, grad, spread, rim_in, forms, pick, normals, pairs, leaving,
    load_sem, out_sem, send_sem, recv_sem, edge_send, edge_recv,
    ) = scratch
    sub_count = lax.axis_size("sub")
    me = lax.axis_index("dom") * sub_count + lax.axis_index("sub")

    def device(k):
        to = lax.rem(me + k, DEVICES)
        return to, (lax.div(to, sub_count), lax.rem(to, sub_count))

    loads = [
        pltpu.make_async_copy(src, dst, load_sem.at[i])
        for i, (src, dst) in enumerate(zip(inputs, held))
    ]
    for copy in loads:
        copy.start()
    barrier = pltpu.get_barrier_semaphore()

    def greet(k, _):
        pl.semaphore_signal(barrier, inc=1, device_id=device(k)[1], device_id_type=MESH)
        return 0

    lax.fori_loop(1, DEVICES, greet, 0)
    for copy in loads[:3]:
        copy.wait()
    ranks(owner_ref, rank_ref, run, tri)
    place(owner_ref, rank_ref, pos_ref, vel_ref, going, acc)
    pl.semaphore_wait(barrier, DEVICES - 1)

    def edges(i, first, last, land):
        pair = []
        for end, (src, k) in enumerate(((last, 1), (first, DEVICES - 1))):
            copy = pltpu.make_async_remote_copy(
                src, land.at[end], edge_send.at[i, end], edge_recv.at[i, end],
                device_id=device(k)[1], device_id_type=MESH,
            )
            copy.start()
            pair.append(copy)
        return pair

    def tile(i):
        return pl.ds(pl.multiple_of(8 * i, 8), 8)

    def exchange(i, src, dst):
        def send(k, _):
            to, where = device(k)
            pltpu.make_async_remote_copy(
                src.at[tile(to)], dst.at[tile(me)], send_sem.at[i], recv_sem.at[i],
                device_id=where, device_id_type=MESH,
            ).start()
            return 0

        lax.fori_loop(1, DEVICES, send, 0)
        dst[tile(me), :] = src[tile(me), :]
        others = pl.ds(0, (DEVICES - 1) * 8)
        return pltpu.make_async_remote_copy(
            src.at[others], dst.at[others], send_sem.at[i], recv_sem.at[i],
            device_id=device(1)[1], device_id_type=MESH,
        )

    halo = edges(0, vel_ref.at[:, 0:HALO], vel_ref.at[:, NODE_DEV - HALO : NODE_DEV], vel_in)
    nodes_move = exchange(0, going, coming)
    for copy in loads[3:]:
        copy.wait()
    face_rows(center_ref, angle_ref, stiff_ref, angles, unit, faces)
    lend(list_ref, faces, lent)
    ghosts = edges(1, lent.at[:, 0:GHOST], lent.at[:, GHOST : 2 * GHOST], ghost_in)
    unpack(vel_ref, conn_in, grad_in, stress_in, vel, conn, grad, stress)
    for copy in halo:
        copy.wait()
    vel[pl.ds(0, 5, stride=EXT), :] = vel_in[0]
    vel[pl.ds(ROWS + 1, 5, stride=EXT), :] = vel_in[1]
    elements(vel, conn, grad, area_ref, thick_ref, limit_ref, stress, spread)
    leave = [
        pltpu.make_async_copy(src, dst, out_sem.at[i])
        for i, (src, dst) in enumerate(((stress, cells_hbm), (total, total_hbm)))
    ]
    leave[0].start()
    for copy in ghosts:
        copy.wait()
    faces[:, 0:GHOST] = jnp.where(me > 0, ghost_in[0], 0.0)
    faces[:, GHOST + FACE_DEV :] = jnp.where(me < DEVICES - 1, ghost_in[1], 0.0)
    face_tables(faces, forms, pick, normals)
    nodes_move.wait()

    tiles = coming.reshape(DEVICES, 8, 128)

    def pair_step(b, _):
        first = b * PAIR_STEP
        forces = []
        for i in range(PAIR_STEP):
            x, f = tiles[node_ref[first + i]], face_of_ref[first + i]
            forces.append(pair_force(x, forms[f], lambda c, k, f=f: normals[f, c, k : k + 8]))
        for i, force in enumerate(forces):
            for c in range(3):
                pairs[pl.ds(c * PAIRS + first + i, 1), :] = force[c]
        return 0

    lax.fori_loop(0, PAIRS // PAIR_STEP, pair_step, 0)
    slot = lax.broadcasted_iota(jnp.int32, (1, PAIRS), 1)
    listed = onehot(DEVICES, jnp.where(slot < count_ref[...], node_row_ref[...], -1))
    listed = jnp.concatenate([listed] * 3, axis=1)
    leaving[...] = jnp.zeros_like(leaving)
    for c in range(3):
        parts = jnp.concatenate(split(pairs[c * PAIRS : (c + 1) * PAIRS, :], 3), axis=0)
        leaving[pl.ds(c, DEVICES, stride=8), :] = dot(listed, parts, NN)
    forces_move = exchange(1, leaving, back)

    sum_ref[...] = jnp.zeros_like(sum_ref)
    last = NODE_DEV // 256 - 1
    scatter_blocks([0, last, *range(1, SPREAD_STEP - 1)], conn_in, spread, sum_ref)
    rims = edges(
        2, sum_ref.at[:, 0:HALO], sum_ref.at[:, HALO + NODE_DEV : 2 * HALO + NODE_DEV], rim_in
    )

    def scatter_step(b, _):
        first = b * SPREAD_STEP - 1
        scatter_blocks([first + i for i in range(SPREAD_STEP)], conn_in, spread, sum_ref)
        return 0

    lax.fori_loop(1, NODE_DEV // (256 * SPREAD_STEP), scatter_step, 0)
    for copy in rims:
        copy.wait()
    sum_ref[:, HALO : 2 * HALO] += rim_in[0]
    sum_ref[:, NODE_DEV : NODE_DEV + HALO] += rim_in[1]
    forces_move.wait()
    totals(back, owner_ref, rank_ref, sum_ref, total, side)
    leave[1].start()
    for copy in leave:
        copy.wait()


def totals(back_ref, owner_ref, rank_ref, sum_ref, out_ref, side):
    for c in range(3):
        turned = back_ref[pl.ds(c, DEVICES, stride=8), :].T
        for i, part in enumerate(split(turned, 2)):
            side[128 * c : 128 * c + 128, 128 * i : 128 * i + 128] = part

    def block(b):
        at = lane_aligned(b, 256)
        own = onehot(DEVICES, owner_ref[0:1, at])
        found = dot(side[...], jnp.concatenate([own, own], axis=0), NN)
        rank = rank_ref[0:1, at].astype(jnp.int32)
        mine = lax.broadcasted_iota(jnp.int32, (128, 256), 0) == rank
        contact = [
            jnp.sum(jnp.where(mine, found[128 * c : 128 * c + 128], 0.0), axis=0, keepdims=True)
            for c in range(3)
        ]
        contact = jnp.concatenate([*contact, jnp.zeros((2, 256), F32)], axis=0)
        return contact - sum_ref[0:5, pl.ds(pl.multiple_of(b * 256 + HALO, HALO), 256)]

    def step(b, _):
        done = [block(b * FINISH_STEP + i) for i in range(FINISH_STEP)]
        for i, value in enumerate(done):
            out_ref[:, lane_aligned(b * FINISH_STEP + i, 256)] = value
        return 0

    lax.fori_loop(0, NODE_DEV // (256 * FINISH_STEP), step, 0)


def finish_kernel(
    total_hbm, vel_hbm, mass_hbm, cells_hbm, out_hbm, new_hbm, total, vel, mass, cells, out, new,
    in_sem, out_sem,
):
    inside = [
        pltpu.make_async_copy(src, dst, in_sem.at[i])
        for i, (src, dst) in enumerate(
            ((cells_hbm, cells), (total_hbm, total), (vel_hbm, vel), (mass_hbm, mass))
        )
    ]
    for copy in inside:
        copy.start()
    inside[0].wait()

    def pack(j, _):
        at = lane_aligned(j, 128)
        for layer in range(5):
            new[layer, :, at] = cells[pl.ds(layer * 5 * ROWS + j, 5, stride=ROWS), :]
        return 0

    lax.fori_loop(0, ROWS, pack, 0, unroll=8)
    outside = [pltpu.make_async_copy(new, new_hbm, out_sem.at[0])]
    outside[0].start()
    for copy in inside[1:]:
        copy.wait()
    out[...] = vel[...] + mass[...] * total[...]
    outside.append(pltpu.make_async_copy(out, out_hbm, out_sem.at[1]))
    outside[1].start()
    for copy in outside:
        copy.wait()


def body(
    velocity, position, inv_mass, connectivity, shape_grad, area, thickness, yield_stress, stress,
    contact_owner, face_center, face_angle, face_stiffness, ghost_list, pair_node, pair_face,
    pair_count,
):
    square = (ROWS, 128)
    owner = contact_owner.reshape(1, NODE_DEV)
    hbm = pl.BlockSpec(memory_space=pltpu.HBM)
    args = (
        owner, position, velocity, face_center, face_angle, face_stiffness.reshape(1, FACE_DEV),
        ghost_list.reshape(1, 2 * GHOST), connectivity, shape_grad, stress, area.reshape(square),
        thickness.reshape(square), yield_stress.reshape(square), pair_node, pair_face,
        pair_node.reshape(1, PAIRS), pair_count.reshape(1, 1),
    )
    held = [
        (pltpu.SMEM if len(arg.shape) == 1 else pltpu.VMEM)(arg.shape, arg.dtype) for arg in args
    ]
    dma = pltpu.SemaphoreType.DMA
    scratch = [
        ((DEVICES * 8, 128), F32), ((8, NODE_DEV + 2 * HALO), F32), ((1, NODE_DEV), F32),
        ((25 * ROWS, 128), F32), ((5, NODE_DEV), F32), ((3 * 128, 256), BF),
        ((DEVICES, 128), F32), ((448, 256), F32), ((256, 384), BF),
        ((DEVICES * 8, 128), F32), ((DEVICES * 8, 128), F32), ((FACE_DEV // 64, 128), F32),
        ((FACE_DEV // 16, 128), F32), ((8, FACE_TILES * 128), F32), ((8, 2 * GHOST), F32),
        ((2, 8, GHOST), F32), ((2, 5, HALO), F32), ((5 * EXT, 128), F32),
        ((4 * ROWS, 128), jnp.int32), ((8 * ROWS, 128), F32), ((4, 8 * ROWS, 128), F32),
        ((2, 8, HALO), F32), ((FACE_TILES, 3 * TILE, 48), BF), ((24, 3 * TILE), BF),
        ((FACE_TILES, 3, TILE, TILE), F32), ((3 * PAIRS, 128), F32), ((DEVICES * 8, 128), F32),
    ]
    total, cells = pl.pallas_call(
        step_kernel,
        out_shape=(
            jax.ShapeDtypeStruct((5, NODE_DEV), F32),
            jax.ShapeDtypeStruct((25 * ROWS, 128), F32),
        ),
        in_specs=[hbm] * len(args),
        out_specs=(hbm, hbm),
        scratch_shapes=[
            *held,
            *(pltpu.VMEM(shape, kind) for shape, kind in scratch),
            dma((len(args),)), dma((2,)), dma((2,)), dma((2,)), dma((3, 2)), dma((3, 2)),
        ],
        compiler_params=pltpu.CompilerParams(
            vmem_limit_bytes=56 * 2**20, collective_id=0, has_side_effects=True
        ),
        name="crash_step",
    )(*args)
    last = (total, velocity, inv_mass.reshape(1, NODE_DEV), cells)
    results = (
        jax.ShapeDtypeStruct((5, NODE_DEV), F32),
        jax.ShapeDtypeStruct((5, 5, NODE_DEV), F32),
    )
    return pl.pallas_call(
        finish_kernel,
        out_shape=results,
        in_specs=[hbm] * len(last),
        out_specs=(hbm, hbm),
        scratch_shapes=[
            *(pltpu.VMEM(x.shape, x.dtype) for x in (*last, *results)), dma((len(last),)), dma((2,)),
        ],
        compiler_params=pltpu.CompilerParams(vmem_limit_bytes=56 * 2**20),
        name="finish",
    )(*last)


def solution(mesh):
    axes = ("dom", "sub")
    nodes, rows, cells = P(axes), P(None, axes), P(None, None, axes)
    in_specs = (
        rows, rows, nodes, rows, cells, nodes, nodes, nodes, cells, P(axes, None), rows, rows,
        nodes, nodes, nodes, nodes, nodes,
    )
    return jax.shard_map(
        body, mesh=mesh, in_specs=in_specs, out_specs=(rows, cells), check_vma=False
    )
```

time: 66.5 us -> 48.5 us (0.73)
  the two profiles are of different devices: /device:TPU:0 before, /device:TPU:1 now
where the time goes in v3:
time: 48.5 us; the launch traced here: 48.4 us
  Pallas kernels  47.1 us (97%)
  between operations  1.29 us (3%)
    pallas_call x1, Pallas kernels, body(): pl.pallas_call(step_kernel, out_shape=(jax.ShapeDtypeStruct((5, NODE_DEV)...  44.2 us
    pallas_call x1, Pallas kernels, body(): pl.pallas_call(finish_kernel, out_shape=results, in_specs=[hbm] * len(las...  2.89 us

profile of v3, /device:TPU:1, one launch (start us, length us, event | category | flops | bytes accessed | tf_op | source)
XLA Modules:
  0.0 48.4 jit_solution(1170834237446337249)
XLA Ops:
  1.3 44.2 %crash_step.1 = (f32[5,8192]{1,0:T(8,128)}, f32[1600,128]{1,0:T(8,128)}) custom-call(s32[1,8192]{1,0:T(1,128)} %bitcast.10, f32[3,8192]{1,0:T(4,128)} %refs_1_.1, f32[5,8192]{1,0:T(8,128)} %vel_hbm.1, f32[3,2048]{1,0:T(4,128)} %refs_3_.1, f32[2,2048]{1,0:T(2,128)} %refs_4_.1, f32[1,2048]{1,0:T(1,128)} %bitcast.15, s32[1,512]{1,0:T(1,128)} %bitcast.16, ...), custom_call_target="tpu_custom_call" | custom-call | tf_op jit(solution)/shard_map/crash_step/pallas_call | solution.py:566
  45.5 2.9 %finish.1 = (f32[5,8192]{1,0:T(8,128)}, f32[5,5,8192]{2,1,0:T(8,128)}) custom-call(f32[5,8192]{1,0:T(8,128)} %get-tuple-element.4.total_hbm, f32[5,8192]{1,0:T(8,128)} %vel_hbm.1, f32[1,8192]{1,0:T(1,128)} %bitcast.14, f32[1600,128]{1,0:T(8,128)} %get-tuple-element.5.cells_hbm), custom_call_target="tpu_custom_call" | custom-call | tf_op jit(solution)/shard_map/finish/pallas_call | solution.py:589

commit v4 on v3

--- a/solution.py
+++ b/solution.py
@@ -57,7 +57,7 @@
 
 
 MESH = pl.DeviceIdType.MESH
-RANK_STEP, PLACE_STEP, SPREAD_STEP, FACE_STEP, PAIR_STEP, FINISH_STEP = 8, 4, 8, 10, 8, 8
+RANK_STEP, PLACE_STEP, SPREAD_STEP, FACE_STEP, PAIR_STEP, FINISH_STEP = 8, 4, 8, 10, 16, 8
 PARTS = (3, 3, 3, 2, 2, 2, 1)
 
 
@@ -341,9 +341,9 @@
     ) = held
     total_hbm, cells_hbm = outputs
     (
-        back, sum_ref, rank_ref, stress, total, side, run, acc, tri, going, coming, angles, unit, faces, lent, ghost_in,
-    vel_in, vel, conn, grad, spread, rim_in, forms, pick, normals, pairs, leaving,
-    load_sem, out_sem, send_sem, recv_sem, edge_send, edge_recv,
+        back, sum_ref, rank_ref, stress, total, side, run, acc, tri, going, coming, angles, unit,
+        faces, lent, ghost_in, vel_in, vel, conn, grad, spread, rim_in, forms, pick, normals, pairs,
+        leaving, load_sem, out_sem, send_sem, recv_sem, edge_send, edge_recv,
     ) = scratch
     sub_count = lax.axis_size("sub")
     me = lax.axis_index("dom") * sub_count + lax.axis_index("sub")
@@ -358,6 +358,7 @@
     ]
     for copy in loads:
         copy.start()
+    coming[pl.ds(7, DEVICES, stride=8), :] = jnp.ones((DEVICES, 128), F32)
     barrier = pltpu.get_barrier_semaphore()
 
     def greet(k, _):
@@ -385,25 +386,28 @@
     def tile(i):
         return pl.ds(pl.multiple_of(8 * i, 8), 8)
 
-    def exchange(i, src, dst):
+    def exchange(i, src, dst, rows):
+        def part(t):
+            return pl.ds(pl.multiple_of(8 * t, 8), rows)
+
         def send(k, _):
             to, where = device(k)
             pltpu.make_async_remote_copy(
-                src.at[tile(to)], dst.at[tile(me)], send_sem.at[i], recv_sem.at[i],
+                src.at[part(to)], dst.at[part(me)], send_sem.at[i], recv_sem.at[i],
                 device_id=where, device_id_type=MESH,
             ).start()
             return 0
 
         lax.fori_loop(1, DEVICES, send, 0)
         dst[tile(me), :] = src[tile(me), :]
-        others = pl.ds(0, (DEVICES - 1) * 8)
+        others = pl.ds(0, (DEVICES - 1) * rows)
         return pltpu.make_async_remote_copy(
             src.at[others], dst.at[others], send_sem.at[i], recv_sem.at[i],
             device_id=device(1)[1], device_id_type=MESH,
         )
 
     halo = edges(0, vel_ref.at[:, 0:HALO], vel_ref.at[:, NODE_DEV - HALO : NODE_DEV], vel_in)
-    nodes_move = exchange(0, going, coming)
+    nodes_move = exchange(0, going, coming, 7)
     for copy in loads[3:]:
         copy.wait()
     face_rows(center_ref, angle_ref, stiff_ref, angles, unit, faces)
@@ -448,7 +452,7 @@
     for c in range(3):
         parts = jnp.concatenate(split(pairs[c * PAIRS : (c + 1) * PAIRS, :], 3), axis=0)
         leaving[pl.ds(c, DEVICES, stride=8), :] = dot(listed, parts, NN)
-    forces_move = exchange(1, leaving, back)
+    forces_move = exchange(1, leaving, back, 3)
 
     sum_ref[...] = jnp.zeros_like(sum_ref)
     last = NODE_DEV // 256 - 1
@@ -506,30 +510,27 @@
     total_hbm, vel_hbm, mass_hbm, cells_hbm, out_hbm, new_hbm, total, vel, mass, cells, out, new,
     in_sem, out_sem,
 ):
-    inside = [
-        pltpu.make_async_copy(src, dst, in_sem.at[i])
-        for i, (src, dst) in enumerate(
-            ((cells_hbm, cells), (total_hbm, total), (vel_hbm, vel), (mass_hbm, mass))
-        )
+    size = 5 * ROWS
+    moves = [(total_hbm, total), (vel_hbm, vel), (mass_hbm, mass)]
+    moves += [
+        (cells_hbm.at[pl.ds(i * size, size)], cells.at[pl.ds(i * size, size)]) for i in range(5)
     ]
+    inside = [pltpu.make_async_copy(*move, in_sem.at[i]) for i, move in enumerate(moves)]
     for copy in inside:
         copy.start()
-    inside[0].wait()
-
-    def pack(j, _):
-        at = lane_aligned(j, 128)
-        for layer in range(5):
-            new[layer, :, at] = cells[pl.ds(layer * 5 * ROWS + j, 5, stride=ROWS), :]
-        return 0
-
-    lax.fori_loop(0, ROWS, pack, 0, unroll=8)
-    outside = [pltpu.make_async_copy(new, new_hbm, out_sem.at[0])]
+    for copy in inside[:3]:
+        copy.wait()
+    out[...] = vel[...] + mass[...] * total[...]
+    outside = [pltpu.make_async_copy(out, out_hbm, out_sem.at[5])]
     outside[0].start()
-    for copy in inside[1:]:
-        copy.wait()
-    out[...] = vel[...] + mass[...] * total[...]
-    outside.append(pltpu.make_async_copy(out, out_hbm, out_sem.at[1]))
-    outside[1].start()
+    for layer in range(5):
+        inside[3 + layer].wait()
+        for j in range(ROWS):
+            part = cells[pl.ds(layer * size + j, 5, stride=ROWS), :]
+            new[layer, :, 128 * j : 128 * j + 128] = part
+        copy = pltpu.make_async_copy(new.at[layer], new_hbm.at[layer], out_sem.at[layer])
+        copy.start()
+        outside.append(copy)
     for copy in outside:
         copy.wait()
 
@@ -592,7 +593,7 @@
         in_specs=[hbm] * len(last),
         out_specs=(hbm, hbm),
         scratch_shapes=[
-            *(pltpu.VMEM(x.shape, x.dtype) for x in (*last, *results)), dma((len(last),)), dma((2,)),
+            *(pltpu.VMEM(x.shape, x.dtype) for x in (*last, *results)), dma((8,)), dma((6,)),
         ],
         compiler_params=pltpu.CompilerParams(vmem_limit_bytes=56 * 2**20),
         name="finish",

time: 48.5 us -> 44.1 us (0.909)
  Pallas kernels: 47.1 us -> 42.7 us
    pallas_call x1, Pallas kernels: 44.2 us -> 40.2 us  [body(): pl.pallas_call(step_kernel, out_shape=(jax.ShapeDtypeStruct((5, NODE_DEV)...]
where the time goes in v4:
time: 44.1 us; the launch traced here: 44 us
  Pallas kernels  42.7 us (97%)
  between operations  1.29 us (3%)
    pallas_call x1, Pallas kernels, body(): pl.pallas_call(step_kernel, out_shape=(jax.ShapeDtypeStruct((5, NODE_DEV)...  40.2 us
    pallas_call x1, Pallas kernels, body(): pl.pallas_call(finish_kernel, out_shape=results, in_specs=[hbm] * len(las...  2.44 us

profile of v4, /device:TPU:1, one launch (start us, length us, event | category | flops | bytes accessed | tf_op | source)
XLA Modules:
  0.0 44.0 jit_solution(12251771550205851335)
XLA Ops:
  1.3 40.2 %crash_step.1 = (f32[5,8192]{1,0:T(8,128)}, f32[1600,128]{1,0:T(8,128)}) custom-call(s32[1,8192]{1,0:T(1,128)} %bitcast.10, f32[3,8192]{1,0:T(4,128)} %refs_1_.1, f32[5,8192]{1,0:T(8,128)} %vel_hbm.1, f32[3,2048]{1,0:T(4,128)} %refs_3_.1, f32[2,2048]{1,0:T(2,128)} %refs_4_.1, f32[1,2048]{1,0:T(1,128)} %bitcast.15, s32[1,512]{1,0:T(1,128)} %bitcast.16, ...), custom_call_target="tpu_custom_call" | custom-call | tf_op jit(solution)/shard_map/crash_step/pallas_call | solution.py:567
  41.5 2.4 %finish.1 = (f32[5,8192]{1,0:T(8,128)}, f32[5,5,8192]{2,1,0:T(8,128)}) custom-call(f32[5,8192]{1,0:T(8,128)} %get-tuple-element.4.total_hbm, f32[5,8192]{1,0:T(8,128)} %vel_hbm.1, f32[1,8192]{1,0:T(1,128)} %bitcast.14, f32[1600,128]{1,0:T(8,128)} %get-tuple-element.5.cells_hbm), custom_call_target="tpu_custom_call" | custom-call | tf_op jit(solution)/shard_map/finish/pallas_call | solution.py:590

commit v5 on v4

--- a/solution.py
+++ b/solution.py
@@ -1,4 +1,4 @@
-import functools
+import itertools
 
 import jax
 import jax.numpy as jnp
@@ -57,8 +57,8 @@
 
 
 MESH = pl.DeviceIdType.MESH
-RANK_STEP, PLACE_STEP, SPREAD_STEP, FACE_STEP, PAIR_STEP, FINISH_STEP = 8, 4, 8, 10, 16, 8
-PARTS = (3, 3, 3, 2, 2, 2, 1)
+RANK_STEP, PLACE_STEP, SPREAD_STEP, FACE_STEP, PAIR_STEP, FINISH_STEP = 16, 4, 8, 10, 16, 8
+PARTS = (2, 2, 2, 2, 2, 2, 1)
 
 
 def constitutive(corner, grad_x, grad_y, area, thickness, limit, old):
@@ -333,6 +333,14 @@
     return [scale * jnp.sum(t, axis=0, keepdims=True) for t in total]
 
 
+def reach(offset):
+    z, y, core, x = offset
+    return sum(min(d, 4 - d) for d in (z, y, x)) + 0.5 * core
+
+
+OFFSETS = sorted(itertools.product(range(4), range(4), range(2), range(4)), key=reach)[:0:-1]
+
+
 def step_kernel(*refs):
     inputs, outputs, held, scratch = refs[:17], refs[17:19], refs[19:36], refs[36:]
     (
@@ -352,6 +360,15 @@
         to = lax.rem(me + k, DEVICES)
         return to, (lax.div(to, sub_count), lax.rem(to, sub_count))
 
+    digits = (lax.div(me, 32), lax.rem(lax.div(me, 8), 4), lax.rem(lax.div(me, 4), 2), lax.rem(me, 4))
+
+    def device_at(offset):
+        z, y, core, x = (
+            lax.rem(digit + step, size) for digit, step, size in zip(digits, offset, (4, 4, 2, 4))
+        )
+        group = (z * 4 + y) * 2 + core
+        return group * 4 + x, (group, x)
+
     loads = [
         pltpu.make_async_copy(src, dst, load_sem.at[i])
         for i, (src, dst) in enumerate(zip(inputs, held))
@@ -390,15 +407,13 @@
         def part(t):
             return pl.ds(pl.multiple_of(8 * t, 8), rows)
 
-        def send(k, _):
-            to, where = device(k)
+        for offset in OFFSETS:
+            to, where = device_at(offset)
             pltpu.make_async_remote_copy(
                 src.at[part(to)], dst.at[part(me)], send_sem.at[i], recv_sem.at[i],
                 device_id=where, device_id_type=MESH,
             ).start()
-            return 0
-
-        lax.fori_loop(1, DEVICES, send, 0)
+
         dst[tile(me), :] = src[tile(me), :]
         others = pl.ds(0, (DEVICES - 1) * rows)
         return pltpu.make_async_remote_copy(

time: 44.1 us -> 42.2 us (0.957)
  Pallas kernels: 42.7 us -> 40.8 us
    pallas_call x1, Pallas kernels: 40.2 us -> 38.4 us  [body(): pl.pallas_call(step_kernel, out_shape=(jax.ShapeDtypeStruct((5, NODE_DEV)...]
where the time goes in v5:
time: 42.2 us; the launch traced here: 42.1 us
  Pallas kernels  40.8 us (97%)
  between operations  1.29 us (3%)
    pallas_call x1, Pallas kernels, body(): pl.pallas_call(step_kernel, out_shape=(jax.ShapeDtypeStruct((5, NODE_DEV)...  38.4 us
    pallas_call x1, Pallas kernels, body(): pl.pallas_call(finish_kernel, out_shape=results, in_specs=[hbm] * len(las...  2.44 us

profile of v5, /device:TPU:1, one launch (start us, length us, event | category | flops | bytes accessed | tf_op | source)
XLA Modules:
  0.0 42.1 jit_solution(13395233360317130356)
XLA Ops:
  1.3 38.4 %crash_step.1 = (f32[5,8192]{1,0:T(8,128)}, f32[1600,128]{1,0:T(8,128)}) custom-call(s32[1,8192]{1,0:T(1,128)} %bitcast.10, f32[3,8192]{1,0:T(4,128)} %refs_1_.1, f32[5,8192]{1,0:T(8,128)} %vel_hbm.1, f32[3,2048]{1,0:T(4,128)} %refs_3_.1, f32[2,2048]{1,0:T(2,128)} %refs_4_.1, f32[1,2048]{1,0:T(1,128)} %bitcast.15, s32[1,512]{1,0:T(1,128)} %bitcast.16, ...), custom_call_target="tpu_custom_call" | custom-call | tf_op jit(solution)/shard_map/crash_step/pallas_call | solution.py:582
  39.6 2.4 %finish.1 = (f32[5,8192]{1,0:T(8,128)}, f32[5,5,8192]{2,1,0:T(8,128)}) custom-call(f32[5,8192]{1,0:T(8,128)} %get-tuple-element.4.total_hbm, f32[5,8192]{1,0:T(8,128)} %vel_hbm.1, f32[1,8192]{1,0:T(1,128)} %bitcast.14, f32[1600,128]{1,0:T(8,128)} %get-tuple-element.5.cells_hbm), custom_call_target="tpu_custom_call" | custom-call | tf_op jit(solution)/shard_map/finish/pallas_call | solution.py:605

commit v6 on v5

--- a/solution.py
+++ b/solution.py
@@ -303,9 +303,9 @@
         depth = [*(-strength * v for v in m), none, none, none, none, strength * apart]
         along = [none, none, none, *(-DAMPING * v for v in m), none, jnp.ones_like(apart)]
         reach = [*((2.0 / REACH_SQ * LOG2E) * v for v in r), none, none, none, none, none]
-        for i, form in enumerate((depth, along, reach)):
-            terms = six_terms(jnp.concatenate(form, axis=0))
-            forms[f, TILE * i : TILE * i + TILE, :] = terms.T.astype(BF)
+        terms = [six_terms(jnp.concatenate(form, axis=0)) for form in (depth, along, reach)]
+        forms[f, 0:TILE, :] = jnp.concatenate(terms[:2], axis=0).T.astype(BF)
+        forms[f, TILE : 2 * TILE, 0:48] = terms[2].T.astype(BF)
         parts = [part.astype(F32) for part in split(jnp.concatenate([*m] + [none] * 5, axis=0), 3)]
         wide = dot(jnp.concatenate(parts, axis=0).T.astype(BF), pick[...], NN)
         for i in range(3):
@@ -321,14 +321,18 @@
 
 def pair_force(x, form, normal_of):
     high, mid, low = split(x, 3)
-    products = dot(form, jnp.concatenate([high, high, mid, mid, high, low], axis=0), NN)
+    node = jnp.concatenate([high, high, mid, mid, high, low], axis=0)
+    none = jnp.zeros_like(node)
+    both = [jnp.concatenate(two, axis=1) for two in ((node, none), (none, node))]
+    products = dot(form[0:TILE], jnp.concatenate(both, axis=0), NN)
+    reach = dot(form[TILE : 2 * TILE, 0:48], node, NN)
     square = x[0:1] * x[0:1] + x[1:2] * x[1:2] + x[2:3] * x[2:3]
     scale = x[6:7] * jnp.exp2((-LOG2E / REACH_SQ) * square)
     total = [jnp.zeros((8, TILE), F32) for _ in range(3)]
     for k in range(0, TILE, 8):
-        depth = jnp.maximum(products[k : k + 8], 0.0)
-        along = products[TILE + k : TILE + k + 8]
-        size = depth * along * jnp.exp2(products[2 * TILE + k : 2 * TILE + k + 8])
+        depth = jnp.maximum(products[k : k + 8, 0:TILE], 0.0)
+        along = products[k : k + 8, TILE : 2 * TILE]
+        size = depth * along * jnp.exp2(reach[k : k + 8])
         total = [t + size * normal_of(i, k) for i, t in enumerate(total)]
     return [scale * jnp.sum(t, axis=0, keepdims=True) for t in total]
 
@@ -576,7 +580,7 @@
         ((FACE_DEV // 16, 128), F32), ((8, FACE_TILES * 128), F32), ((8, 2 * GHOST), F32),
         ((2, 8, GHOST), F32), ((2, 5, HALO), F32), ((5 * EXT, 128), F32),
         ((4 * ROWS, 128), jnp.int32), ((8 * ROWS, 128), F32), ((4, 8 * ROWS, 128), F32),
-        ((2, 8, HALO), F32), ((FACE_TILES, 3 * TILE, 48), BF), ((24, 3 * TILE), BF),
+        ((2, 8, HALO), F32), ((FACE_TILES, 2 * TILE, 96), BF), ((24, 3 * TILE), BF),
         ((FACE_TILES, 3, TILE, TILE), F32), ((3 * PAIRS, 128), F32), ((DEVICES * 8, 128), F32),
     ]
     total, cells = pl.pallas_call(

time: 42.2 us -> 40.9 us (0.969)
  Pallas kernels: 40.8 us -> 39.5 us
    pallas_call x1, Pallas kernels: 38.4 us -> 37 us  [body(): pl.pallas_call(step_kernel, out_shape=(jax.ShapeDtypeStruct((5, NODE_DEV)...]
where the time goes in v6:
time: 40.9 us; the launch traced here: 40.8 us
  Pallas kernels  39.5 us (97%)
  between operations  1.29 us (3%)
    pallas_call x1, Pallas kernels, body(): pl.pallas_call(step_kernel, out_shape=(jax.ShapeDtypeStruct((5, NODE_DEV)...  37 us
    pallas_call x1, Pallas kernels, body(): pl.pallas_call(finish_kernel, out_shape=results, in_specs=[hbm] * len(las...  2.44 us

profile of v6, /device:TPU:1, one launch (start us, length us, event | category | flops | bytes accessed | tf_op | source)
XLA Modules:
  0.0 40.8 jit_solution(799201445525733181)
XLA Ops:
  1.3 37.0 %crash_step.1 = (f32[5,8192]{1,0:T(8,128)}, f32[1600,128]{1,0:T(8,128)}) custom-call(s32[1,8192]{1,0:T(1,128)} %bitcast.10, f32[3,8192]{1,0:T(4,128)} %refs_1_.1, f32[5,8192]{1,0:T(8,128)} %vel_hbm.1, f32[3,2048]{1,0:T(4,128)} %refs_3_.1, f32[2,2048]{1,0:T(2,128)} %refs_4_.1, f32[1,2048]{1,0:T(1,128)} %bitcast.15, s32[1,512]{1,0:T(1,128)} %bitcast.16, ...), custom_call_target="tpu_custom_call" | custom-call | tf_op jit(solution)/shard_map/crash_step/pallas_call | solution.py:586
  38.3 2.4 %finish.1 = (f32[5,8192]{1,0:T(8,128)}, f32[5,5,8192]{2,1,0:T(8,128)}) custom-call(f32[5,8192]{1,0:T(8,128)} %get-tuple-element.4.total_hbm, f32[5,8192]{1,0:T(8,128)} %vel_hbm.1, f32[1,8192]{1,0:T(1,128)} %bitcast.14, f32[1600,128]{1,0:T(8,128)} %get-tuple-element.5.cells_hbm), custom_call_target="tpu_custom_call" | custom-call | tf_op jit(solution)/shard_map/finish/pallas_call | solution.py:609

commit v7 on v6

--- a/solution.py
+++ b/solution.py
@@ -353,7 +353,7 @@
     ) = held
     total_hbm, cells_hbm = outputs
     (
-        back, sum_ref, rank_ref, stress, total, side, run, acc, tri, going, coming, angles, unit,
+        back, sum_ref, rank_ref, stress, total, side, hots, run, acc, tri, going, coming, angles, unit,
         faces, lent, ghost_in, vel_in, vel, conn, grad, spread, rim_in, forms, pick, normals, pairs,
         leaving, load_sem, out_sem, send_sem, recv_sem, edge_send, edge_recv,
     ) = scratch
@@ -490,14 +490,24 @@
         copy.wait()
     sum_ref[:, HALO : 2 * HALO] += rim_in[0]
     sum_ref[:, NODE_DEV : NODE_DEV + HALO] += rim_in[1]
+    owner_onehots(owner_ref, hots)
     forces_move.wait()
-    totals(back, owner_ref, rank_ref, sum_ref, total, side)
+    totals(back, hots, rank_ref, sum_ref, total, side)
     leave[1].start()
     for copy in leave:
         copy.wait()
 
 
-def totals(back_ref, owner_ref, rank_ref, sum_ref, out_ref, side):
+def owner_onehots(owner_ref, hots):
+    def step(b, _):
+        at = lane_aligned(b, 1024)
+        hots[:, at] = onehot(DEVICES, owner_ref[0:1, at])
+        return 0
+
+    lax.fori_loop(0, NODE_DEV // 1024, step, 0)
+
+
+def totals(back_ref, hots, rank_ref, sum_ref, out_ref, side):
     for c in range(3):
         turned = back_ref[pl.ds(c, DEVICES, stride=8), :].T
         for i, part in enumerate(split(turned, 2)):
@@ -505,7 +515,7 @@
 
     def block(b):
         at = lane_aligned(b, 256)
-        own = onehot(DEVICES, owner_ref[0:1, at])
+        own = hots[:, at]
         found = dot(side[...], jnp.concatenate([own, own], axis=0), NN)
         rank = rank_ref[0:1, at].astype(jnp.int32)
         mine = lax.broadcasted_iota(jnp.int32, (128, 256), 0) == rank
@@ -574,7 +584,7 @@
     dma = pltpu.SemaphoreType.DMA
     scratch = [
         ((DEVICES * 8, 128), F32), ((8, NODE_DEV + 2 * HALO), F32), ((1, NODE_DEV), F32),
-        ((25 * ROWS, 128), F32), ((5, NODE_DEV), F32), ((3 * 128, 256), BF),
+        ((25 * ROWS, 128), F32), ((5, NODE_DEV), F32), ((3 * 128, 256), BF), ((DEVICES, NODE_DEV), BF),
         ((DEVICES, 128), F32), ((448, 256), F32), ((256, 384), BF),
         ((DEVICES * 8, 128), F32), ((DEVICES * 8, 128), F32), ((FACE_DEV // 64, 128), F32),
         ((FACE_DEV // 16, 128), F32), ((8, FACE_TILES * 128), F32), ((8, 2 * GHOST), F32),

time: 40.9 us -> 40.7 us (level)
  no operation moved by 1% of the time
where the time goes in v7:
time: 40.7 us; the launch traced here: 40.4 us
  Pallas kernels  39.1 us (96%)
  between operations  1.29 us (3%)
    pallas_call x1, Pallas kernels, body(): pl.pallas_call(step_kernel, out_shape=(jax.ShapeDtypeStruct((5, NODE_DEV)...  36.7 us
    pallas_call x1, Pallas kernels, body(): pl.pallas_call(finish_kernel, out_shape=results, in_specs=[hbm] * len(las...  2.44 us

profile of v7, /device:TPU:1, one launch (start us, length us, event | category | flops | bytes accessed | tf_op | source)
XLA Modules:
  0.0 40.4 jit_solution(181413874128722096)
XLA Ops:
  1.3 36.7 %crash_step.1 = (f32[5,8192]{1,0:T(8,128)}, f32[1600,128]{1,0:T(8,128)}) custom-call(s32[1,8192]{1,0:T(1,128)} %bitcast.10, f32[3,8192]{1,0:T(4,128)} %refs_1_.1, f32[5,8192]{1,0:T(8,128)} %vel_hbm.1, f32[3,2048]{1,0:T(4,128)} %refs_3_.1, f32[2,2048]{1,0:T(2,128)} %refs_4_.1, f32[1,2048]{1,0:T(1,128)} %bitcast.15, s32[1,512]{1,0:T(1,128)} %bitcast.16, ...), custom_call_target="tpu_custom_call" | custom-call | tf_op jit(solution)/shard_map/crash_step/pallas_call | solution.py:596
  38.0 2.4 %finish.1 = (f32[5,8192]{1,0:T(8,128)}, f32[5,5,8192]{2,1,0:T(8,128)}) custom-call(f32[5,8192]{1,0:T(8,128)} %get-tuple-element.4.total_hbm, f32[5,8192]{1,0:T(8,128)} %vel_hbm.1, f32[1,8192]{1,0:T(1,128)} %bitcast.14, f32[1600,128]{1,0:T(8,128)} %get-tuple-element.5.cells_hbm), custom_call_target="tpu_custom_call" | custom-call | tf_op jit(solution)/shard_map/finish/pallas_call | solution.py:619
